TPU v7x, 256 devices: a whole 4x4x8 slice. The times are simulated.
256 devices in a mesh: tile: 64 (over y, z, core), grp: 4 (over x).
Axes of the slice: x: 4, y: 4, z: 8, core: 2. Of those that a mesh axis runs over, the one named last changes fastest.
Arguments:
- noisy: bfloat16 [4, 7, 4096, 256], P(None, None, ('tile', 'grp')), may hold values from -6 to 6
- state_0: bfloat16 [32, 4096, 256], P(None, ('tile', 'grp')), may hold values from -6 to 6
- state_1: bfloat16 [43, 2048, 128], P(None, ('tile', 'grp')), may hold values from -6 to 6
- state_2: bfloat16 [57, 1024, 64], P(None, ('tile', 'grp')), may hold values from -6 to 6
- state_3: bfloat16 [76, 512, 32], P(None, ('tile', 'grp')), may hold values from -6 to 6
- state_4: bfloat16 [101, 256, 16], P(None, ('tile', 'grp')), may hold values from -6 to 6
- enc_in_0: bfloat16 [9, 32, 7], replicated, may hold values from -0.75 to 0.75
- enc_in_1: bfloat16 [9, 43, 32], replicated, may hold values from -0.375 to 0.375
- enc_in_2: bfloat16 [9, 57, 43], replicated, may hold values from -0.3125 to 0.3125
- enc_in_3: bfloat16 [9, 76, 57], replicated, may hold values from -0.25 to 0.25
- enc_in_4: bfloat16 [9, 101, 76], replicated, may hold values from -0.21875 to 0.21875
- enc_rec_0: bfloat16 [9, 32, 64], replicated, may hold values from -0.375 to 0.375
- enc_rec_1: bfloat16 [9, 43, 86], replicated, may hold values from -0.3125 to 0.3125
- enc_rec_2: bfloat16 [9, 57, 114], replicated, may hold values from -0.25 to 0.25
- enc_rec_3: bfloat16 [9, 76, 152], replicated, may hold values from -0.21875 to 0.21875
- enc_rec_4: bfloat16 [9, 101, 202], replicated, may hold values from -0.1875 to 0.1875
- dec_0: bfloat16 [9, 32, 75], replicated, may hold values from -0.25 to 0.25
- dec_1: bfloat16 [9, 43, 100], replicated, may hold values from -0.1875 to 0.1875
- dec_2: bfloat16 [9, 57, 133], replicated, may hold values from -0.1875 to 0.1875
- dec_3: bfloat16 [9, 76, 177], replicated, may hold values from -0.15625 to 0.15625
- out_weight: bfloat16 [9, 3, 32], replicated, may hold values from -0.375 to 0.375
Outputs:
- denoised: float32 [4, 3, 4096, 256], P(None, None, ('tile', 'grp'))
- final_state: bfloat16 [101, 256, 16], P(None, ('tile', 'grp'))
All inputs are finite; a program needn't handle non-finite values.
Results may differ from a plain program's by a relative error of at most 0.025.
Values may be sent and summed in bfloat16 or wider, within the bound.
No kernel may reach another device: no remote copies, remote signals or barrier semaphores. Data moves between devices by JAX's collectives and lax.ppermute only.
A program may use at most 64 MiB of HBM per device.

v0:
```python
import functools

import jax
import jax.numpy as jnp
import numpy as np
from jax import lax
from jax.experimental import pallas as pl
from jax.experimental.pallas import tpu as pltpu
from jax.sharding import PartitionSpec as P

BF = jnp.bfloat16
F32 = jnp.float32
AXES = ("tile", "grp")
FRAMES = 4
C0, C1, C2, C3, C4 = 32, 48, 64, 80, 112
X_AT = (C2, C2 + C1 + 48, C2 + 2 * C1 + 48, C2 + 3 * C1 + 48)
REST_AT = C2 + C1
BLOCK = C2 + 48 + FRAMES * C1
PREFIX = (X_AT[0] + C1, X_AT[1] + C1, X_AT[2] + C1, X_AT[3] + C1)
VMEM = 56 * 1024 * 1024
GROUP = 12
GROUP2 = 6


SHAPES = {
    "rec0": (C0, 2, ((32, C0), (32, C0))),
    "in1": (C1, 1, ((32, C0),)),
    "rec1": (C1, 1, ((43, C1), (43, C1))),
    "in2": (C2, 1, ((43, C1),)),
    "rec2": (C2, 1, ((57, C2), (57, C2))),
    "in3": (C3, 1, ((57, C2),)),
    "rec3": (C3, 1, ((76, C3), (76, C3))),
    "in4": (C4, 1, ((76, C3),)),
    "rec4": (C4, 1, ((101, C4), (101, C4))),
    "dec3": (C3, 1, ((101, C4), (76, C3))),
    "dec2": (C2, 1, ((76, C3), (57, C2))),
    "dec1": (C1, 1, ((57, C2), (43, C1))),
    "dec0": (C0, 1, ((43, C1), (32, C0))),
    "out": (8, 4, ((32, C0),)),
}


def taps_shape(name):
    if name == "in0":
        return (4 * C0, 144)
    pad, rows, parts = SHAPES[name]
    return (rows * 3 * pad, (rows + 2) * sum(p for _, p in parts))


def weights_kernel(*refs):
    count = len(SHAPES) + 1
    work = refs[-1]
    for name, raw, done in zip(("in0",) + tuple(SHAPES), refs[:count], refs[count:-1]):
        high, wide = taps_shape(name)
        work[:high, :wide] = jnp.zeros((high, wide), F32)
        o = raw.shape[1]
        for t in range(9):
            dr, dw = divmod(t, 3)
            k = raw[t].astype(F32)
            if name == "in0":
                for m in range(4):
                    p, odd = divmod(m + dr, 2)
                    at = p * 48 + dw * 16 + odd * 8
                    work[m * C0 : m * C0 + o, at : at + 7] = k
                continue
            pad, rows, parts = SHAPES[name]
            depth = sum(p for _, p in parts)
            for m in range(rows):
                row, at, first = (m * 3 + dw) * pad, (m + dr) * depth, 0
                for chans, wide_part in parts:
                    work[row : row + o, at : at + chans] = k[:, first : first + chans]
                    at += wide_part
                    first += chans
        done[...] = work[:high, :wide].astype(BF)


def pool_matrix(width, rows, lane_of):
    m = np.zeros((rows * width, 256), np.float32)
    for r in range(0, rows, 2):
        for c in range(0, width, 2):
            m[r * width + c, lane_of(r // 2, c // 2)] = 1
    return m


def selections():
    out = {}
    s0 = np.zeros((256, 128), np.float32)
    s0[2 * np.arange(128), np.arange(128)] = 1
    out["s0"] = s0
    s1 = np.zeros((4, 128, 256), np.float32)
    for j in range(4):
        s1[j, 2 * np.arange(64), 64 * j + np.arange(64)] = 1
    out["s1"] = s1.reshape(512, 256)
    out["s2"] = np.concatenate(
        [pool_matrix(64, 4, lambda r, c, i=i: 64 * i + 32 * r + c) for i in range(4)], 0
    )
    out["s3"] = np.concatenate(
        [pool_matrix(32, 8, lambda r, c, i=i: 64 * i + 16 * r + c) for i in range(4)], 0
    )
    u3 = np.zeros((256, 256), np.float32)
    for r in range(-4, 4):
        for c in range(32):
            u3[(r // 2 + 8) * 16 + c // 2, (r + 4) * 32 + c] = 1
    out["u3"] = u3
    u2 = np.zeros((256, 768), np.float32)
    for r in range(-4, 8):
        if -4 <= r // 2 < 4:
            for c in range(64):
                u2[(r // 2 + 4) * 32 + c // 2, (r + 4) * 64 + c] = 1
    out["u2"] = u2
    u1 = np.zeros((256, 512), np.float32)
    for r in range(4):
        for c in range(128):
            u1[r * 64 + c // 2, r * 128 + c] = 1
    out["u1"] = u1
    u0 = np.zeros((128, 256), np.float32)
    u0[np.arange(256) // 2, np.arange(256)] = 1
    out["u0"] = u0
    return {k: jnp.asarray(v, BF) for k, v in out.items()}


def dot(a, b):
    return jnp.dot(a, b, preferred_element_type=F32)


def lanes(shape):
    return lax.broadcasted_iota(jnp.int32, shape, 1)


def join_columns(y, out, width):
    count = y.shape[1]
    col = lanes((out, count)) & (width - 1)
    left = pltpu.roll(y[:out], 1, 1)
    right = pltpu.roll(y[2 * out :], count - 1, 1)
    return (
        y[out : 2 * out]
        + jnp.where(col == 0, 0.0, left)
        + jnp.where(col == width - 1, 0.0, right)
    )


def act(u):
    return jnp.maximum(u, 0.1 * u)


def three_rows(before, here, after, width):
    here32 = here.astype(F32)
    lane = lanes(here.shape)
    up = jnp.where(
        lane < width, pltpu.roll(before.astype(F32), width, 1), pltpu.roll(here32, width, 1)
    )
    down = jnp.where(
        lane >= 256 - width,
        pltpu.roll(after.astype(F32), 256 - width, 1),
        pltpu.roll(here32, 256 - width, 1),
    )
    return jnp.concatenate([up.astype(BF), here, down.astype(BF)], 0)


def three_rows_alone(here, width):
    here32 = here.astype(F32)
    up = pltpu.roll(here32, width, 1).astype(BF)
    down = pltpu.roll(here32, 256 - width, 1).astype(BF)
    return jnp.concatenate([up, here, down], 0)


def pair_max(value, width):
    count = value.shape[1]
    value = jnp.maximum(value, pltpu.roll(value, count - 1, 1))
    return jnp.maximum(value, pltpu.roll(value, count - width, 1))


def rounds(count, body, group):
    def run(first, size):
        for store in [body(first + j) for j in range(size)]:
            store()

    full = count // group

    def step(i, carry):
        run(i * group, group)
        return carry

    lax.fori_loop(0, full, step, 0)
    if count % group:
        run(full * group, count % group)


def fine_kernel(
    pos, own, up, down, rest, t_in0, t_rec0, t_in1, t_rec1, s0, s1,
    block, skip0, skip1, n, xs0, m0, x1, xs1,
):
    dev = pos[0]
    has_up = (dev > 0).astype(F32)
    has_down = (dev < 255).astype(F32)

    def place(src, part):
        lane = lanes((16, 256))
        for f in range(FRAMES):

            def columns(i, f=f):
                here = src[pl.ds(pl.multiple_of(f * 128 + 16 * i, 16), 16)]
                wide = here.astype(F32)
                left = jnp.where(lane == 0, 0.0, pltpu.roll(wide, 1, 1)).astype(BF)
                right = jnp.where(lane == 255, 0.0, pltpu.roll(wide, 255, 1)).astype(BF)

                def store():
                    n[f, part * 8 + i, :16] = left
                    n[f, part * 8 + i, 16:32] = here
                    n[f, part * 8 + i, 32:] = right

                return store

            rounds(8, columns, 8)
        xs0[0, part * 16 : part * 16 + 16, C0:] = src[512:1024].reshape(16, C0, 256)
        for j in range(4):
            two = src[1024 + j * C1 : 1024 + (j + 1) * C1]
            xs1[0, part * 8 + 2 * j, C1:] = two[:, :128]
            xs1[0, part * 8 + 2 * j + 1, C1:] = two[:, 128:]

    place(up, 0)
    place(own, 1)
    place(down, 2)

    for f in range(FRAMES):
        n[f, 24] = jnp.zeros((48, 256), BF)
    block[:C2] = rest[:C2]
    block[REST_AT : REST_AT + 48] = rest[C2:]

    for f in range(FRAMES):
        now, new = f % 2, (f + 1) % 2
        halo = 14 - 2 * f

        def in0(i, f=f, now=now, halo=halo):
            r = 16 - (halo + 1) + 4 * i
            p = (r - 1) // 2
            v = act(dot(t_in0[...], n[f, pl.ds(p, 3)].reshape(144, 256)))
            rows = []
            for m in range(4):
                row = r + m
                keep = jnp.where(row < 16, has_up, jnp.where(row >= 32, has_down, 1.0))
                rows.append((v[m * C0 : m * C0 + C0] * keep).astype(BF))

            def store():
                for m in range(4):
                    xs0[now, r + m, :C0] = rows[m]

            return store

        rounds((8 + halo + 2) // 2, in0, GROUP // 2)

        def rec0(i, f=f, now=now, new=new, halo=halo):
            r = 16 - halo + 2 * i
            rhs = xs0[now, pl.ds(r - 1, 4)].reshape(256, 256)
            y = dot(t_rec0[...], rhs)
            keep = jnp.where(r < 16, has_up, jnp.where(r >= 32, has_down, 1.0))
            both = []
            for m in range(2):
                v = act(join_columns(y[m * 96 : m * 96 + 96], C0, 256)) * keep
                both.append(v)
            top = jnp.maximum(both[0], both[1])
            top = jnp.maximum(top, pltpu.roll(top, 255, 1)).astype(BF)

            def store():
                for m in range(2):
                    xs0[new, r + m, C0:] = both[m].astype(BF)
                m0[i] = top

            return store

        rounds(8 + halo, rec0, GROUP)

        skip0[f] = xs0[new, 14:34, C0:]
        count = 8 + halo
        x1[:count] = dot(m0[:count].reshape(count * C0, 256), s0[...]).astype(BF).reshape(
            count, C0, 128
        )

        half = 5 - f

        def in1(i, f=f, now=now, half=half):
            left = x1[pl.ds(2 * i, 3)].reshape(3 * C0, 128)
            right = x1[pl.ds(2 * i + 1, 3)].reshape(3 * C0, 128)
            y = dot(t_in1[...], jnp.concatenate([left, right], 1))
            v = act(join_columns(y, C1, 128))
            both = []
            for m in range(2):
                row = 8 - (half + 1) + 2 * i + m
                keep = jnp.where(row < 8, has_up, jnp.where(row >= 16, has_down, 1.0))
                both.append((v[:, m * 128 : m * 128 + 128] * keep).astype(BF))

            def store():
                for m in range(2):
                    xs1[now, 8 - (half + 1) + 2 * i + m, :C1] = both[m]

            return store

        rounds(4 + half + 1, in1, GROUP)

        def rec1(i, f=f, now=now, new=new, half=half):
            r = 8 - half + 2 * i
            left = xs1[now, pl.ds(r - 1, 3)].reshape(6 * C1, 128)
            right = xs1[now, pl.ds(r, 3)].reshape(6 * C1, 128)
            y = dot(t_rec1[...], jnp.concatenate([left, right], 1))
            v = act(join_columns(y, C1, 128))
            both = []
            for m in range(2):
                row = r + m
                keep = jnp.where(row < 8, has_up, jnp.where(row >= 16, has_down, 1.0))
                both.append((v[:, m * 128 : m * 128 + 128] * keep).astype(BF))

            def store():
                for m in range(2):
                    xs1[new, r + m, C1:] = both[m]

            return store

        rounds(4 + half, rec1, GROUP)

        skip1[f] = xs1[new, 6:18, C1:]
        pooled = []
        for j in range(4):
            a = xs1[new, 8 + 2 * j, C1:].astype(F32)
            b = xs1[new, 9 + 2 * j, C1:].astype(F32)
            top = jnp.maximum(a, b)
            pooled.append(jnp.maximum(top, pltpu.roll(top, 127, 1)).astype(BF))
        block[X_AT[f] : X_AT[f] + C1] = dot(jnp.concatenate(pooled, 1), s1[...]).astype(BF)


def deep_kernel(
    pos, own, up1, down1, up2, down2, skip0, skip1,
    t_in2, t_rec2, t_in3, t_rec3, t_in4, t_rec4,
    t_dec3, t_dec2, t_dec1, t_dec0, t_out,
    s2, s3, u3, u2, u1, u0,
    out, final,
    w, xa2, xa3, x3, xa4, xd1, xd0, d0, keep4, keep3, keep2,
):
    dev, g = pos[0], pos[1]
    has_up = (dev > 0).astype(F32)
    has_down = (dev < 255).astype(F32)
    zero_block = jnp.zeros((BLOCK, 256), BF)
    w[0] = zero_block
    w[21] = zero_block
    w[5:9] = up1[...]
    w[9:13] = own[...]
    w[13:17] = down1[...]
    at = 0
    for d in range(4):
        size = PREFIX[d]
        for slot, src in ((1 + d, up2), (20 - d, down2)):
            w[slot, :size] = src[at : at + size]
            if size < BLOCK:
                w[slot, size:] = jnp.zeros((BLOCK - size, 256), BF)
        at += size

    def init2(i, carry):
        xa2[0, i, C2:] = w[i + g, :C2]
        xa2[1, i] = jnp.zeros((2 * C2, 256), BF)
        return carry

    lax.fori_loop(0, 19, init2, 0)
    for part in range(2):
        xa3[part, 0] = jnp.zeros((2 * C3, 256), BF)
        xa3[part, 5] = jnp.zeros((2 * C3, 256), BF)
    x3[0] = jnp.zeros((C2, 256), BF)
    x3[5] = jnp.zeros((C2, 256), BF)

    lane48 = lanes((48, 256))
    for b in range(4):
        low = jnp.zeros((48, 256), F32)
        high = jnp.zeros((48, 256), F32)
        for i in range(4):
            src = w[4 * b - 8 + i + 9 + g, REST_AT : REST_AT + 48].astype(F32)
            here = (lane48 >= 64 * i) & (lane48 < 64 * i + 64)
            low = jnp.where(here, pltpu.roll(src, 64 * i, 1) if i else src, low)
            shift = (64 * i - 128) % 256
            high = jnp.where(here, pltpu.roll(src, shift, 1) if shift else src, high)
        xa3[0, b + 1, C3 : C3 + 48] = low.astype(BF)
        xa3[0, b + 1, C3 + 48 :] = high[:32].astype(BF)
    low = jnp.zeros((48, 256), F32)
    high = jnp.zeros((48, 256), F32)
    top = jnp.zeros((16, 256), F32)
    for k in range(-6, 7):
        src = w[k + 9 + g, REST_AT : REST_AT + 48].astype(F32)
        first = 16 * (k + 8)
        here = (lane48 >= first) & (lane48 < first + 16)
        low = jnp.where(here, pltpu.roll(src, (first - 64) % 256, 1), low)
        high = jnp.where(here, pltpu.roll(src, (first - 192) % 256, 1), high)
        top = jnp.where(here[:16], pltpu.roll(src[:16], (first - 80) % 256, 1), top)
    xa4[C4 : C4 + 48] = low.astype(BF)
    xa4[C4 + 48 : C4 + 96] = high.astype(BF)
    xa4[C4 + 96 :] = top.astype(BF)

    lane1 = lanes((1, 256))

    def in_image(first, lane_device):
        d = dev + first + lane_device
        return ((d >= 0) & (d < 256)).astype(F32)

    mask3 = [in_image(4 * b - 8, lane1 // 64) for b in range(4)]
    mask4 = in_image(-8, lane1 // 16)
    mask3d = in_image(-2, lane1 // 64)

    for f in range(FRAMES):
        now, new = f % 2, (f + 1) % 2

        def in2(i, f=f, now=now):
            k = i - (8 - f)
            rows = slice(X_AT[f], X_AT[f] + C1)
            p = k + 9 + g
            rhs = three_rows(w[p - 1, rows], w[p, rows], w[p + 1, rows], 64)
            v = act(join_columns(dot(t_in2[...], rhs), C2, 64))
            keep = ((dev + k >= 0) & (dev + k < 256)).astype(F32)
            v = (v * keep).astype(BF)

            def store():
                xa2[now, k + 9, :C2] = v

            return store

        rounds(17 - 2 * f, in2, GROUP2)

        def rec2(i, f=f, now=now, new=new):
            k = i - (7 - f)
            p = k + 9
            rhs = three_rows(xa2[now, p - 1], xa2[now, p], xa2[now, p + 1], 64)
            v = act(join_columns(dot(t_rec2[...], rhs), C2, 64))
            keep = ((dev + k >= 0) & (dev + k < 256)).astype(F32)
            v = (v * keep).astype(BF)

            def store():
                xa2[new, p, C2:] = v

            return store

        rounds(15 - 2 * f, rec2, GROUP2)

        for b in range(4):
            pooled = [
                pair_max(xa2[new, 4 * b - 8 + i + 9, C2:].astype(F32), 64).astype(BF)
                for i in range(4)
            ]
            x3[b + 1] = dot(jnp.concatenate(pooled, 1), s2[...]).astype(BF)

        for b in range(1 if f == 3 else 0, 4):
            rhs = three_rows(x3[b], x3[b + 1], x3[b + 2], 32)
            v = act(join_columns(dot(t_in3[...], rhs), C3, 32))
            xa3[now, b + 1, :C3] = (v * mask3[b]).astype(BF)
        for b in range((0, 0, 1, 1)[f], (4, 4, 4, 3)[f]):
            rhs = three_rows(xa3[now, b], xa3[now, b + 1], xa3[now, b + 2], 32)
            v = act(join_columns(dot(t_rec3[...], rhs), C3, 32))
            xa3[new, b + 1, C3:] = (v * mask3[b]).astype(BF)

        pooled = [pair_max(xa3[new, b + 1, C3:].astype(F32), 32).astype(BF) for b in range(4)]
        x4 = dot(jnp.concatenate(pooled, 1), s3[...]).astype(BF)

        v = act(join_columns(dot(t_in4[...], three_rows_alone(x4, 16)), C4, 16))
        xa4[:C4] = (v * mask4).astype(BF)
        v = act(join_columns(dot(t_rec4[...], three_rows_alone(xa4[...], 16)), C4, 16))
        s4 = (v * mask4).astype(BF)
        xa4[C4:] = s4
        if f == FRAMES - 1:
            final[...] = s4

        keep4[f] = s4
        keep3[f] = jnp.concatenate([xa3[new, 2, C3:][:, 128:], xa3[new, 3, C3:][:, :128]], 1)
        for k in range(3):
            keep2[f, k] = xa2[new, 8 + k, C2:]

    every = range(FRAMES)
    d3 = []
    for f in every:
        both = jnp.concatenate([dot(keep4[f], u3[...]).astype(BF), keep3[f]], 0)
        v = act(join_columns(dot(t_dec3[...], three_rows_alone(both, 32)), C3, 32))
        d3.append((v * mask3d).astype(BF))

    d2 = []
    for f in every:
        up = dot(d3[f], u2[...]).astype(BF)
        parts = [
            jnp.concatenate([up[:, 256 * j : 256 * j + 256], keep2[f, j]], 0) for j in range(3)
        ]
        for j in range(3):
            rhs = three_rows(parts[max(j - 1, 0)], parts[j], parts[min(j + 1, 2)], 64)
            v = act(join_columns(dot(t_dec2[...], rhs), C2, 64))
            keep = (has_up, 1.0, has_down)[j]
            d2.append((v * keep).astype(BF))

    for f in every:
        up = dot(jnp.concatenate(d2[3 * f : 3 * f + 3], 0), u1[...]).astype(BF)
        for j, low, high, first in ((0, 3, 4, 0), (1, 0, 4, 2), (2, 0, 1, 10)):
            for r in range(low, high):
                row = first + 2 * (r - low)
                piece = up[j * C2 : j * C2 + C2, 128 * r : 128 * r + 128]
                xd1[f, row, :C2] = piece
                xd1[f, row + 1, :C2] = piece
        xd1[f, :, C2:] = skip1[f]

    d1 = [[] for f in every]
    for f in every:
        for i in range(5):
            left = xd1[f, 2 * i : 2 * i + 3].reshape(3 * (C1 + C2), 128)
            right = xd1[f, 2 * i + 1 : 2 * i + 4].reshape(3 * (C1 + C2), 128)
            v = act(join_columns(dot(t_dec1[...], jnp.concatenate([left, right], 1)), C1, 128))
            first, second = v[:, :128], v[:, 128:]
            if i == 0:
                first = first * has_up
            if i == 4:
                second = second * has_down
            d1[f] += [first.astype(BF), second.astype(BF)]

    for f in every:
        up = dot(jnp.concatenate(d1[f], 0), u0[...]).astype(BF)
        for j in range(10):
            piece = up[j * C1 : j * C1 + C1]
            xd0[f, 2 * j, :C1] = piece
            xd0[f, 2 * j + 1, :C1] = piece
        xd0[f, :, C1:] = skip0[f]

    for f in every:

        def dec0(i, f=f):
            rhs = xd0[f, pl.ds(i, 3)].reshape(3 * (C0 + C1), 256)
            v = act(join_columns(dot(t_dec0[...], rhs), C0, 256))
            keep = jnp.where(i == 0, has_up, jnp.where(i == 17, has_down, 1.0))
            v = (v * keep).astype(BF)

            def store():
                d0[f, i] = v

            return store

        rounds(18, dec0, 18)

    for f in every:
        done = []
        for r in range(0, 16, 4):
            y = dot(t_out[...], d0[f, r : r + 6].reshape(6 * C0, 256))
            done += [join_columns(y[24 * m : 24 * m + 24], 8, 256) for m in range(4)]
        for r in range(16):
            for o in range(3):
                out[f, o, r : r + 1, :] = done[r][o : o + 1]


def pack_kernel(tile, up, down):
    at = 0
    for i, size in enumerate(PREFIX):
        up[at : at + size] = tile[i, :size]
        down[at : at + size] = tile[3 - i, :size]
        at += size


def shifted(value, axis, by):
    peers = lax.axis_size(axis)
    pairs = [(i, i + by) for i in range(peers) if 0 <= i + by < peers]
    return lax.ppermute(value, axis, pairs)


def per_device(
    noisy, state_0, state_1, state_2, state_3, state_4,
    enc_in_0, enc_in_1, enc_in_2, enc_in_3, enc_in_4,
    enc_rec_0, enc_rec_1, enc_rec_2, enc_rec_3, enc_rec_4,
    dec_0, dec_1, dec_2, dec_3, out_weight,
):
    grp = lax.axis_index("grp")
    dev = lax.axis_index("tile") * lax.axis_size("grp") + grp
    pos = jnp.stack([dev, grp]).astype(jnp.int32)

    own = jnp.concatenate(
        [
            jnp.pad(noisy.transpose(0, 2, 1, 3), ((0, 0), (0, 0), (0, 1), (0, 0))).reshape(512, 256),
            state_0.transpose(1, 0, 2).reshape(512, 256),
            jnp.pad(state_1.reshape(43, 4, 2, 128).transpose(1, 0, 2, 3), ((0, 0), (0, 5), (0, 0), (0, 0))).reshape(4 * C1, 256),
        ],
        0,
    )
    up = shifted(own, AXES, 1)
    down = shifted(own, AXES, -1)

    three = jnp.pad(state_3.reshape(76, 64), ((0, 20), (0, 0))).reshape(2, 48, 64)
    four = jnp.pad(state_4.reshape(101, 16), ((0, 43), (0, 0))).reshape(3, 48, 16)
    gap = jnp.zeros((48, 32), BF)
    rest = jnp.concatenate(
        [
            jnp.pad(state_2.reshape(57, 256), ((0, 7), (0, 0))),
            jnp.concatenate([three[0], four[0], four[2], gap, three[1], four[1], gap, gap[:, :16]], 1),
        ],
        0,
    )

    sel = selections()
    smem = pl.BlockSpec(memory_space=pltpu.SMEM)
    vmem = pl.BlockSpec(memory_space=pltpu.VMEM)
    params = pltpu.CompilerParams(vmem_limit_bytes=VMEM)

    raw = (
        enc_in_0, enc_rec_0, enc_in_1, enc_rec_1, enc_in_2, enc_rec_2, enc_in_3, enc_rec_3,
        enc_in_4, enc_rec_4, dec_3, dec_2, dec_1, dec_0, out_weight,
    )
    names = ("in0",) + tuple(SHAPES)
    (
        t_in0, t_rec0, t_in1, t_rec1, t_in2, t_rec2, t_in3, t_rec3,
        t_in4, t_rec4, t_dec3, t_dec2, t_dec1, t_dec0, t_out,
    ) = pl.pallas_call(
        weights_kernel,
        out_shape=[jax.ShapeDtypeStruct(taps_shape(name), BF) for name in names],
        scratch_shapes=[pltpu.VMEM((384, 768), F32)],
        cost_estimate=pl.CostEstimate(flops=0, bytes_accessed=20_000_000, transcendentals=0),
        compiler_params=params,
        name="weights",
    )(*raw)

    block, skip0, skip1 = pl.pallas_call(
        fine_kernel,
        out_shape=(
            jax.ShapeDtypeStruct((BLOCK, 256), BF),
            jax.ShapeDtypeStruct((FRAMES, 20, C0, 256), BF),
            jax.ShapeDtypeStruct((FRAMES, 12, C1, 128), BF),
        ),
        in_specs=[smem] + [vmem] * 10,
        out_specs=(vmem, vmem, vmem),
        scratch_shapes=[
            pltpu.VMEM((FRAMES, 25, 48, 256), BF),
            pltpu.VMEM((2, 50, 2 * C0, 256), BF),
            pltpu.VMEM((22, C0, 256), BF),
            pltpu.VMEM((22, C0, 128), BF),
            pltpu.VMEM((2, 24, 2 * C1, 128), BF),
        ],
        compiler_params=params,
        name="fine",
    )(pos, own, up, down, rest, t_in0, t_rec0, t_in1, t_rec1, sel["s0"], sel["s1"])

    tile = lax.all_gather(block, "grp", axis=0)
    up1 = shifted(tile, "tile", 1)
    down1 = shifted(tile, "tile", -1)

    outer = jax.ShapeDtypeStruct((sum(PREFIX), 256), BF)
    send_up, send_down = pl.pallas_call(
        pack_kernel,
        out_shape=(outer, outer),
        compiler_params=params,
        name="pack",
    )(tile)
    up2 = shifted(send_up, "tile", 2)
    down2 = shifted(send_down, "tile", -2)

    denoised, final = pl.pallas_call(
        deep_kernel,
        out_shape=(
            jax.ShapeDtypeStruct((FRAMES, 3, 16, 256), F32),
            jax.ShapeDtypeStruct((C4, 256), BF),
        ),
        in_specs=[smem] + [vmem] * 24,
        out_specs=(vmem, vmem),
        scratch_shapes=[
            pltpu.VMEM((22, BLOCK, 256), BF),
            pltpu.VMEM((2, 19, 2 * C2, 256), BF),
            pltpu.VMEM((2, 6, 2 * C3, 256), BF),
            pltpu.VMEM((6, C2, 256), BF),
            pltpu.VMEM((2 * C4, 256), BF),
            pltpu.VMEM((FRAMES, 12, C1 + C2, 128), BF),
            pltpu.VMEM((FRAMES, 20, C0 + C1, 256), BF),
            pltpu.VMEM((FRAMES, 18, C0, 256), BF),
            pltpu.VMEM((FRAMES, C4, 256), BF),
            pltpu.VMEM((FRAMES, C3, 256), BF),
            pltpu.VMEM((FRAMES, 3, C2, 256), BF),
        ],
        compiler_params=params,
        name="deep",
    )(
        pos, tile, up1, down1, up2, down2, skip0, skip1,
        t_in2, t_rec2, t_in3, t_rec3, t_in4, t_rec4,
        t_dec3, t_dec2, t_dec1, t_dec0, t_out,
        sel["s2"], sel["s3"], sel["u3"], sel["u2"], sel["u1"], sel["u0"],
    )
    return denoised, final[:101, 128:144].reshape(101, 1, 16)


def solution(mesh):
    rows3 = P(None, None, AXES, None)
    rows2 = P(None, AXES, None)
    return jax.shard_map(
        per_device,
        mesh=mesh,
        in_specs=(rows3,) + (rows2,) * 5 + (P(),) * 15,
        out_specs=(rows3, rows2),
        check_vma=False,
    )
```

profile of v0, /device:TPU:106, one launch (start us, length us, event | category | flops | bytes accessed | tf_op | source)
XLA Modules:
  0.0 113.3 jit_solution(2997482651618195169)
XLA Ops:
  0.6 1.1 copy.61
  1.7 1.0 copy.66
  2.7 0.0 copy-start.8
  2.7 0.1 pad.21
  2.8 0.0 copy-start.10
  2.9 0.1 copy.47
  2.9 0.0 copy-start.11
  3.0 0.0 copy-start.12
  3.0 0.0 copy-start.13
  3.0 0.0 copy-start.16
  3.1 0.0 copy-start.17
  3.1 0.0 copy-start.14
  3.1 0.0 copy-start.15
  3.1 3.5 %collective-permute-start = (bf16[1216,256]{1,0:T(8,128)(2,1)S(1)}, bf16[1216,256]{1,0:T(8,128)(2,1)S(1)}, u32[]{:S(2)}, u32[]{:S(2)}) collective-permute-start(bf16[1216,256]{1,0:T(8,128)(2,1)S(1)} %pad_maximum_fusion.own), channel_id=1, source_target_pairs={{0,1},{1,2},{2,3},{3,4},{4,5},{5,6},{6,7},{7,8},{8,9},{9,10},{10,1... | collective-permute-start | bytes 1867784 | tf_op jit(solution)/shard_map/ppermute | solution.py:556
  6.6 2.4 %collective-permute-start.1 = (bf16[1216,256]{1,0:T(8,128)(2,1)S(1)}, bf16[1216,256]{1,0:T(8,128)(2,1)S(1)}, u32[]{:S(2)}, u32[]{:S(2)}) collective-permute-start(bf16[1216,256]{1,0:T(8,128)(2,1)S(1)} %pad_maximum_fusion.own), channel_id=1, source_target_pairs={{1,0},{2,1},{3,2},{4,3},{5,4},{6,5},{7,6},{8,7},{9,8},{10,9},{11,1... | collective-permute-start | bytes 1867784 | tf_op jit(solution)/shard_map/ppermute | solution.py:556
  9.1 1.0 copy.58.refs_7_
  10.1 0.9 copy.59.refs_8_
  11.0 0.9 copy.57.refs_6_
  11.9 0.8 copy.56.refs_4_
  12.7 0.8 copy.55.refs_2_
  13.5 0.8 copy.54.refs_0_
  14.3 0.1 copy.49
  14.4 0.1 copy.51
  14.5 0.1 copy.53
  14.6 0.0 copy-done.15
  14.6 0.1 reshape.47
  14.8 0.1 concatenate.10
  14.9 4.7 %weights.1 = (bf16[128,144]{1,0:T(8,128)(2,1)}, bf16[192,256]{1,0:T(8,128)(2,1)}, bf16[144,96]{1,0:T(8,128)(2,1)}, bf16[144,288]{1,0:T(8,128)(2,1)}, bf16[192,14...) custom-call(bf16[9,32,7]{2,1,0:T(8,128)(2,1)} %copy.54.refs_0_, ...), custom_call_target="tpu_custom_call" | custom-call | bytes 20000000 | tf_op jit(solution)/shard_map/weights/pallas_call | solution.py:604
  19.7 0.6 pad_add_fusion.pos
  20.3 0.6 fusion.1.rest
  20.9 0.0 collective-permute-done.up
  21.0 3.1 %collective-permute-done.1.down = bf16[1216,256]{1,0:T(8,128)(2,1)S(1)} collective-permute-done((bf16[1216,256]{1,0:T(8,128)(2,1)S(1)}, bf16[1216,256]{1,0:T(8,128)(2,1)S(1)}, u32[]{:S(2)}, u32[]{:S(2)}) %collective-permute-start.1) | collective-permute-done | bytes 622624 | tf_op jit(solution)/shard_map/ppermute | solution.py:556
  24.0 0.8 copy-done.5
  24.8 12.0 %fine.1 = (bf16[304,256]{1,0:T(8,128)(2,1)}, bf16[4,20,32,256]{3,2,1,0:T(8,128)(2,1)}, bf16[4,12,48,128]{3,2,1,0:T(8,128)(2,1)}) custom-call(s32[2]{0:T(128)} %pad_add_fusion.pos, bf16[1216,256]{1,0:T(8,128)(2,1)} %copy-done.1, bf16[1216,256]{1,0:T(8,128)(2,1)} %copy-done.4, bf16[1216,256]{1,0:T(8,128)(2,1)} %copy-done.5, bf16[112,256]{1,0:T(8,128)(2,1)} %fusion.1.rest, ...), custom_call_target="tpu_custom_call" | custom-call | tf_op jit(solution)/shard_map/fine/pallas_call | solution.py:613
  36.8 14.4 %all-gather = bf16[1216,256]{1,0:T(8,128)(2,1)S(1)} all-gather(bf16[304,256]{1,0:T(8,128)(2,1)} %get-tuple-element.28), channel_id=2, replica_groups=mesh['tile'=64,'grp'=4] {'grp'}, dimensions={0}, use_global_device_ids=true | all-gather | bytes 778240 | tf_op jit(solution)/shard_map/all_gather | solution.py:633
  51.2 1.9 %collective-permute-start.2 = (bf16[4,304,256]{2,1,0:T(8,128)(2,1)S(1)}, bf16[4,304,256]{2,1,0:T(8,128)(2,1)S(1)}, u32[]{:S(2)}, u32[]{:S(2)}) collective-permute-start(bf16[4,304,256]{2,1,0:T(8,128)(2,1)S(1)} %bitcast.26), channel_id=1, source_target_pairs={{0,4},{4,8},{8,12},{12,16},{16,20},{20,24},{24,28},{28,32},{32,36}... | collective-permute-start | bytes 1867784 | tf_op jit(solution)/shard_map/ppermute | solution.py:556
  53.1 3.6 %collective-permute-start.3 = (bf16[4,304,256]{2,1,0:T(8,128)(2,1)S(1)}, bf16[4,304,256]{2,1,0:T(8,128)(2,1)S(1)}, u32[]{:S(2)}, u32[]{:S(2)}) collective-permute-start(bf16[4,304,256]{2,1,0:T(8,128)(2,1)S(1)} %bitcast.27), channel_id=1, source_target_pairs={{4,0},{8,4},{12,8},{16,12},{20,16},{24,20},{28,24},{32,28},{36,32}... | collective-permute-start | bytes 1867784 | tf_op jit(solution)/shard_map/ppermute | solution.py:556
  56.8 2.1 %pack.1 = (bf16[880,256]{1,0:T(8,128)(2,1)}, bf16[880,256]{1,0:T(8,128)(2,1)}) custom-call(bf16[4,304,256]{2,1,0:T(8,128)(2,1)} %bitcast.28), custom_call_target="tpu_custom_call" | custom-call | tf_op jit(solution)/shard_map/pack/pallas_call | solution.py:638
  58.8 6.3 %collective-permute-start.4 = (bf16[880,256]{1,0:T(8,128)(2,1)}, bf16[880,256]{1,0:T(8,128)(2,1)S(1)}, u32[]{:S(2)}, u32[]{:S(2)}) collective-permute-start(bf16[880,256]{1,0:T(8,128)(2,1)} %get-tuple-element.29), channel_id=1, source_target_pairs={{0,8},{4,12},{8,16},{12,20},{16,24},{20,28},{24,32},{28,36},{32,40... | collective-permute-start | bytes 1351688 | tf_op jit(solution)/shard_map/ppermute | solution.py:556
  65.1 1.9 %collective-permute-start.5 = (bf16[880,256]{1,0:T(8,128)(2,1)}, bf16[880,256]{1,0:T(8,128)(2,1)S(1)}, u32[]{:S(2)}, u32[]{:S(2)}) collective-permute-start(bf16[880,256]{1,0:T(8,128)(2,1)} %get-tuple-element.30), channel_id=1, source_target_pairs={{8,0},{12,4},{16,8},{20,12},{24,16},{28,20},{32,24},{36,28},{40,32... | collective-permute-start | bytes 1351688 | tf_op jit(solution)/shard_map/ppermute | solution.py:556
  67.1 6.9 %collective-permute-done.4.up2 = bf16[880,256]{1,0:T(8,128)(2,1)S(1)} collective-permute-done((bf16[880,256]{1,0:T(8,128)(2,1)}, bf16[880,256]{1,0:T(8,128)(2,1)S(1)}, u32[]{:S(2)}, u32[]{:S(2)}) %collective-permute-start.4) | collective-permute-done | bytes 450592 | tf_op jit(solution)/shard_map/ppermute | solution.py:556
  74.0 4.9 %collective-permute-done.5.down2 = bf16[880,256]{1,0:T(8,128)(2,1)S(1)} collective-permute-done((bf16[880,256]{1,0:T(8,128)(2,1)}, bf16[880,256]{1,0:T(8,128)(2,1)S(1)}, u32[]{:S(2)}, u32[]{:S(2)}) %collective-permute-start.5) | collective-permute-done | bytes 450592 | tf_op jit(solution)/shard_map/ppermute | solution.py:556
  78.9 0.7 copy-done.7
  79.6 0.2 copy-done.2
  79.8 0.2 copy-done.3
  80.0 31.9 %deep.1 = (f32[4,3,16,256]{3,2,1,0:T(8,128)}, bf16[112,256]{1,0:T(8,128)(2,1)}) custom-call(s32[2]{0:T(128)} %pad_add_fusion.pos, bf16[4,304,256]{2,1,0:T(8,128)(2,1)} %bitcast.29, bf16[4,304,256]{2,1,0:T(8,128)(2,1)} %copy-done.2, bf16[4,304,256]{2,1,0:T(8,128)(2,1)} %copy-done.3, bf16[880,256]{1,0:T(8,128)(2,1)} %copy-done.6, bf16[880,256]{1,0:T(8,128)(2,1)} %copy-done.7, ...), custom_call_target="tpu_custom_call" | custom-call | tf_op jit(solution)/shard_map/deep/pallas_call | solution.py:647
  111.9 0.7 slice_bitcast_fusion
  112.7 0.7 copy.60
  (32 shorter events, 0.2 us)
Async XLA Ops:
  0.6 2.2 %copy-start.9 = (bf16[32,16,256]{2,1,0:T(8,128)(2,1)S(1)}, bf16[32,16,256]{2,1,0:T(8,128)(2,1)}, u32[]{:S(2)}) copy-start(bf16[32,16,256]{2,1,0:T(8,128)(2,1)} %param.30) | copy-start | bytes 786436
  2.7 6.4 %copy-start.8 = (bf16[9,76,152]{1,2,0:T(8,128)(2,1)S(1)}, bf16[9,76,152]{1,2,0:T(8,128)(2,1)}, u32[]{:S(2)}) copy-start(bf16[9,76,152]{1,2,0:T(8,128)(2,1)} %param.43) | copy-start | bytes 623812
  2.8 7.3 %copy-start.10 = (bf16[9,101,76]{1,2,0:T(8,128)(2,1)S(1)}, bf16[9,101,76]{1,2,0:T(8,128)(2,1)}, u32[]{:S(2)}) copy-start(bf16[9,101,76]{1,2,0:T(8,128)(2,1)} %param.39) | copy-start | bytes 414508
  2.9 8.1 %copy-start.11 = (bf16[9,76,57]{1,2,0:T(8,128)(2,1)S(1)}, bf16[9,76,57]{1,2,0:T(8,128)(2,1)}, u32[]{:S(2)}) copy-start(bf16[9,76,57]{1,2,0:T(8,128)(2,1)} %param.38) | copy-start | bytes 233932
  3.0 8.9 %copy-start.12 = (bf16[9,57,43]{1,2,0:T(8,128)(2,1)S(1)}, bf16[9,57,43]{1,2,0:T(8,128)(2,1)}, u32[]{:S(2)}) copy-start(bf16[9,57,43]{1,2,0:T(8,128)(2,1)} %param.37) | copy-start | bytes 132358
  3.0 9.8 %copy-start.13 = (bf16[9,43,32]{1,2,0:T(8,128)(2,1)S(1)}, bf16[9,43,32]{1,2,0:T(8,128)(2,1)}, u32[]{:S(2)}) copy-start(bf16[9,43,32]{1,2,0:T(8,128)(2,1)} %param.36) | copy-start | bytes 74308
  3.0 11.9 %copy-start.1 = (bf16[1216,256]{1,0:T(8,128)(2,1)}, bf16[1216,256]{1,0:T(8,128)(2,1)S(1)}, u32[]{:S(2)}) copy-start(bf16[1216,256]{1,0:T(8,128)(2,1)S(1)} %pad_maximum_fusion.own) | copy-start | bytes 1867780
  3.0 10.5 %copy-start.16 = (bf16[9,32,7]{1,2,0:T(8,128)(2,1)S(1)}, bf16[9,32,7]{1,2,0:T(8,128)(2,1)}, u32[]{:S(2)}) copy-start(bf16[9,32,7]{1,2,0:T(8,128)(2,1)} %param.35) | copy-start | bytes 12100
  3.1 11.2 %copy-start.17 = (bf16[101,1,16]{0,2,1:T(8,128)(2,1)S(1)}, bf16[101,1,16]{0,2,1:T(8,128)(2,1)}, u32[]{:S(2)}) copy-start(bf16[101,1,16]{0,2,1:T(8,128)(2,1)} %param.34) | copy-start | bytes 9700
  3.1 11.3 %copy-start.14 = (bf16[76,2,32]{0,2,1:T(8,128)(2,1)S(1)}, bf16[76,2,32]{0,2,1:T(8,128)(2,1)}, u32[]{:S(2)}) copy-start(bf16[76,2,32]{0,2,1:T(8,128)(2,1)} %param.33) | copy-start | bytes 29188
  3.1 11.5 %copy-start.15 = (bf16[57,4,64]{2,1,0:T(4,128)(2,1)S(1)}, bf16[57,4,64]{2,1,0:T(4,128)(2,1)}, u32[]{:S(2)}) copy-start(bf16[57,4,64]{2,1,0:T(4,128)(2,1)} %param.32) | copy-start | bytes 87556
  3.1 17.9 %collective-permute-start = (bf16[1216,256]{1,0:T(8,128)(2,1)S(1)}, bf16[1216,256]{1,0:T(8,128)(2,1)S(1)}, u32[]{:S(2)}, u32[]{:S(2)}) collective-permute-start(bf16[1216,256]{1,0:T(8,128)(2,1)S(1)} %pad_maximum_fusion.own), channel_id=1, source_target_pairs={{0,1},{1,2},{2,3},{3,4},{4,5},{5,6},{6,7},{7,8},{8,9},{9,10},{10,1... | collective-permute-start | bytes 1867784 | tf_op jit(solution)/shard_map/ppermute | solution.py:556
  6.6 17.4 %collective-permute-start.1 = (bf16[1216,256]{1,0:T(8,128)(2,1)S(1)}, bf16[1216,256]{1,0:T(8,128)(2,1)S(1)}, u32[]{:S(2)}, u32[]{:S(2)}) collective-permute-start(bf16[1216,256]{1,0:T(8,128)(2,1)S(1)} %pad_maximum_fusion.own), channel_id=1, source_target_pairs={{1,0},{2,1},{3,2},{4,3},{5,4},{6,5},{7,6},{8,7},{9,8},{10,9},{11,1... | collective-permute-start | bytes 1867784 | tf_op jit(solution)/shard_map/ppermute | solution.py:556
  20.9 3.1 %copy-start.4 = (bf16[1216,256]{1,0:T(8,128)(2,1)}, bf16[1216,256]{1,0:T(8,128)(2,1)S(1)}, u32[]{:S(2)}) copy-start(bf16[1216,256]{1,0:T(8,128)(2,1)S(1)} %collective-permute-done.up) | copy-start | bytes 1867780
  24.0 0.8 copy-start.5
  51.2 5.6 %copy-start = (bf16[1216,256]{1,0:T(8,128)(2,1)}, bf16[1216,256]{1,0:T(8,128)(2,1)S(1)}, u32[]{:S(2)}) copy-start(bf16[1216,256]{1,0:T(8,128)(2,1)S(1)} %all-gather) | copy-start | bytes 1867780
  51.2 27.6 %collective-permute-start.2 = (bf16[4,304,256]{2,1,0:T(8,128)(2,1)S(1)}, bf16[4,304,256]{2,1,0:T(8,128)(2,1)S(1)}, u32[]{:S(2)}, u32[]{:S(2)}) collective-permute-start(bf16[4,304,256]{2,1,0:T(8,128)(2,1)S(1)} %bitcast.26), channel_id=1, source_target_pairs={{0,4},{4,8},{8,12},{12,16},{16,20},{20,24},{24,28},{28,32},{32,36}... | collective-permute-start | bytes 1867784 | tf_op jit(solution)/shard_map/ppermute | solution.py:556
  53.1 25.7 %collective-permute-start.3 = (bf16[4,304,256]{2,1,0:T(8,128)(2,1)S(1)}, bf16[4,304,256]{2,1,0:T(8,128)(2,1)S(1)}, u32[]{:S(2)}, u32[]{:S(2)}) collective-permute-start(bf16[4,304,256]{2,1,0:T(8,128)(2,1)S(1)} %bitcast.27), channel_id=1, source_target_pairs={{4,0},{8,4},{12,8},{16,12},{20,16},{24,20},{28,24},{32,28},{36,32}... | collective-permute-start | bytes 1867784 | tf_op jit(solution)/shard_map/ppermute | solution.py:556
  58.8 15.1 %collective-permute-start.4 = (bf16[880,256]{1,0:T(8,128)(2,1)}, bf16[880,256]{1,0:T(8,128)(2,1)S(1)}, u32[]{:S(2)}, u32[]{:S(2)}) collective-permute-start(bf16[880,256]{1,0:T(8,128)(2,1)} %get-tuple-element.29), channel_id=1, source_target_pairs={{0,8},{4,12},{8,16},{12,20},{16,24},{20,28},{24,32},{28,36},{32,40... | collective-permute-start | bytes 1351688 | tf_op jit(solution)/shard_map/ppermute | solution.py:556
  65.1 13.7 %collective-permute-start.5 = (bf16[880,256]{1,0:T(8,128)(2,1)}, bf16[880,256]{1,0:T(8,128)(2,1)S(1)}, u32[]{:S(2)}, u32[]{:S(2)}) collective-permute-start(bf16[880,256]{1,0:T(8,128)(2,1)} %get-tuple-element.30), channel_id=1, source_target_pairs={{8,0},{12,4},{16,8},{20,12},{24,16},{28,20},{32,24},{36,28},{40,32... | collective-permute-start | bytes 1351688 | tf_op jit(solution)/shard_map/ppermute | solution.py:556
  74.0 4.9 %copy-start.6 = (bf16[880,256]{1,0:T(8,128)(2,1)}, bf16[880,256]{1,0:T(8,128)(2,1)S(1)}, u32[]{:S(2)}) copy-start(bf16[880,256]{1,0:T(8,128)(2,1)S(1)} %collective-permute-done.4.up2) | copy-start | bytes 1351684
  78.8 0.8 copy-start.7
  78.8 1.0 copy-start.2
  78.8 1.2 %copy-start.3 = (bf16[4,304,256]{2,1,0:T(8,128)(2,1)}, bf16[4,304,256]{2,1,0:T(8,128)(2,1)S(1)}, u32[]{:S(2)}) copy-start(bf16[4,304,256]{2,1,0:T(8,128)(2,1)S(1)} %collective-permute-done.3.down1) | copy-start | bytes 1867780
where the time goes:
time: 114 us; the launch traced here: 113 us
  Pallas kernels  50.6 us (44%)
  starting transfers between devices  19.7 us (17%)
  waiting for transfers between devices  14.8 us (13%)
  blocking collectives  14.4 us (13%)
  local copies, waits for them, and re-layouts  11.5 us (10%)
  other arithmetic  1.31 us (1%)
    pallas_call x1, Pallas kernels, per_device(): pl.pallas_call(deep_kernel, out_shape=(jax.ShapeDtypeStruct((FRAMES, 3, 1...  31.9 us
    ppermute x6, starting transfers between devices, shifted(): return lax.ppermute(value, axis, pairs)  19.7 us
    ppermute x6, waiting for transfers between devices, shifted(): return lax.ppermute(value, axis, pairs)  14.8 us
    all_gather x1, blocking collectives, per_device(): tile = lax.all_gather(block, 'grp', axis=0)  14.4 us
    pallas_call x1, Pallas kernels, per_device(): pl.pallas_call(fine_kernel, out_shape=(jax.ShapeDtypeStruct((BLOCK, 256),...  12 us
    unnamed x46, local copies, waits for them, and re-layouts  9.13 us
    pallas_call x1, Pallas kernels, per_device(): pl.pallas_call(weights_kernel, out_shape=[jax.ShapeDtypeStruct(taps_shape...  4.74 us
  transfers between devices with their start and end apart: 6, of which 3 were waited for; matrix products, arithmetic and copies ran while one was open for 6% of the time, Pallas kernels for 6%

commit v1 on v0

--- a/solution.py
+++ b/solution.py
@@ -333,7 +333,7 @@
     t_dec3, t_dec2, t_dec1, t_dec0, t_out,
     s2, s3, u3, u2, u1, u0,
     out, final,
-    w, xa2, xa3, x3, xa4, xd1, xd0, d0, keep4, keep3, keep2,
+    w, xa2, xa3, x3, xa4, xd1, xd0, d0, keep2,
 ):
     dev, g = pos[0], pos[1]
     has_up = (dev > 0).astype(F32)
@@ -353,17 +353,34 @@
                 w[slot, size:] = jnp.zeros((BLOCK - size, 256), BF)
         at += size
 
-    def init2(i, carry):
-        xa2[0, i, C2:] = w[i + g, :C2]
-        xa2[1, i] = jnp.zeros((2 * C2, 256), BF)
-        return carry
-
-    lax.fori_loop(0, 19, init2, 0)
-    for part in range(2):
-        xa3[part, 0] = jnp.zeros((2 * C3, 256), BF)
-        xa3[part, 5] = jnp.zeros((2 * C3, 256), BF)
-    x3[0] = jnp.zeros((C2, 256), BF)
-    x3[5] = jnp.zeros((C2, 256), BF)
+    def spread(buf, slot, first, value):
+        size = value.shape[0]
+        up = pltpu.roll(value, 64, 1).astype(BF)
+        down = pltpu.roll(value, 192, 1).astype(BF)
+        here = 2 * C2 + first
+        below = 4 * C2 + first
+        xa2[buf, slot, first : first + size, 64:] = up[:, 64:]
+        xa2[buf, slot + 1, first : first + size, :64] = up[:, :64]
+        xa2[buf, slot, here : here + size] = value.astype(BF)
+        xa2[buf, slot, below : below + size, :192] = down[:, :192]
+        xa2[buf, slot - 1, below : below + size, 192:] = down[:, 192:]
+
+    def init2(i):
+        value = w[i + g, :C2].astype(F32)
+
+        def store():
+            spread(0, i + 1, C2, value)
+            xa2[1, i + 1, 3 * C2 : 4 * C2] = jnp.zeros((C2, 256), BF)
+
+        return store
+
+    rounds(19, init2, 10)
+    for part in range(FRAMES + 1):
+        for b in range(6):
+            xa3[part, b] = jnp.zeros((2 * C3, 256), BF)
+    for f in range(FRAMES):
+        x3[f, 0] = jnp.zeros((C2, 256), BF)
+        x3[f, 5] = jnp.zeros((C2, 256), BF)
 
     lane48 = lanes((48, 256))
     for b in range(4):
@@ -387,9 +404,9 @@
         low = jnp.where(here, pltpu.roll(src, (first - 64) % 256, 1), low)
         high = jnp.where(here, pltpu.roll(src, (first - 192) % 256, 1), high)
         top = jnp.where(here[:16], pltpu.roll(src[:16], (first - 80) % 256, 1), top)
-    xa4[C4 : C4 + 48] = low.astype(BF)
-    xa4[C4 + 48 : C4 + 96] = high.astype(BF)
-    xa4[C4 + 96 :] = top.astype(BF)
+    xa4[0, C4 : C4 + 48] = low.astype(BF)
+    xa4[0, C4 + 48 : C4 + 96] = high.astype(BF)
+    xa4[0, C4 + 96 :] = top.astype(BF)
 
     lane1 = lanes((1, 256))
 
@@ -411,10 +428,10 @@
             rhs = three_rows(w[p - 1, rows], w[p, rows], w[p + 1, rows], 64)
             v = act(join_columns(dot(t_in2[...], rhs), C2, 64))
             keep = ((dev + k >= 0) & (dev + k < 256)).astype(F32)
-            v = (v * keep).astype(BF)
+            v = v * keep
 
             def store():
-                xa2[now, k + 9, :C2] = v
+                spread(now, k + 10, 0, v)
 
             return store
 
@@ -422,14 +439,13 @@
 
         def rec2(i, f=f, now=now, new=new):
             k = i - (7 - f)
-            p = k + 9
-            rhs = three_rows(xa2[now, p - 1], xa2[now, p], xa2[now, p + 1], 64)
-            v = act(join_columns(dot(t_rec2[...], rhs), C2, 64))
+            p = k + 10
+            v = act(join_columns(dot(t_rec2[...], xa2[now, p]), C2, 64))
             keep = ((dev + k >= 0) & (dev + k < 256)).astype(F32)
-            v = (v * keep).astype(BF)
+            v = v * keep
 
             def store():
-                xa2[new, p, C2:] = v
+                spread(new, p, C2, v)
 
             return store
 
@@ -437,40 +453,41 @@
 
         for b in range(4):
             pooled = [
-                pair_max(xa2[new, 4 * b - 8 + i + 9, C2:].astype(F32), 64).astype(BF)
+                pair_max(xa2[new, 4 * b + i + 2, 3 * C2 : 4 * C2].astype(F32), 64).astype(BF)
                 for i in range(4)
             ]
-            x3[b + 1] = dot(jnp.concatenate(pooled, 1), s2[...]).astype(BF)
-
+            x3[f, b + 1] = dot(jnp.concatenate(pooled, 1), s2[...]).astype(BF)
+        for k in range(3):
+            keep2[f, k] = xa2[new, 9 + k, 3 * C2 : 4 * C2]
+
+    every = range(FRAMES)
+    for f in every:
         for b in range(1 if f == 3 else 0, 4):
-            rhs = three_rows(x3[b], x3[b + 1], x3[b + 2], 32)
+            rhs = three_rows(x3[f, b], x3[f, b + 1], x3[f, b + 2], 32)
             v = act(join_columns(dot(t_in3[...], rhs), C3, 32))
-            xa3[now, b + 1, :C3] = (v * mask3[b]).astype(BF)
+            xa3[f, b + 1, :C3] = (v * mask3[b]).astype(BF)
+    for f in every:
         for b in range((0, 0, 1, 1)[f], (4, 4, 4, 3)[f]):
-            rhs = three_rows(xa3[now, b], xa3[now, b + 1], xa3[now, b + 2], 32)
+            rhs = three_rows(xa3[f, b], xa3[f, b + 1], xa3[f, b + 2], 32)
             v = act(join_columns(dot(t_rec3[...], rhs), C3, 32))
-            xa3[new, b + 1, C3:] = (v * mask3[b]).astype(BF)
-
-        pooled = [pair_max(xa3[new, b + 1, C3:].astype(F32), 32).astype(BF) for b in range(4)]
-        x4 = dot(jnp.concatenate(pooled, 1), s3[...]).astype(BF)
-
-        v = act(join_columns(dot(t_in4[...], three_rows_alone(x4, 16)), C4, 16))
-        xa4[:C4] = (v * mask4).astype(BF)
-        v = act(join_columns(dot(t_rec4[...], three_rows_alone(xa4[...], 16)), C4, 16))
-        s4 = (v * mask4).astype(BF)
-        xa4[C4:] = s4
-        if f == FRAMES - 1:
-            final[...] = s4
-
-        keep4[f] = s4
-        keep3[f] = jnp.concatenate([xa3[new, 2, C3:][:, 128:], xa3[new, 3, C3:][:, :128]], 1)
-        for k in range(3):
-            keep2[f, k] = xa2[new, 8 + k, C2:]
-
-    every = range(FRAMES)
+            xa3[f + 1, b + 1, C3:] = (v * mask3[b]).astype(BF)
+
+    x4 = []
+    for f in every:
+        pooled = [pair_max(xa3[f + 1, b + 1, C3:].astype(F32), 32).astype(BF) for b in range(4)]
+        x4.append(dot(jnp.concatenate(pooled, 1), s3[...]).astype(BF))
+    for f in every:
+        v = act(join_columns(dot(t_in4[...], three_rows_alone(x4[f], 16)), C4, 16))
+        xa4[f, :C4] = (v * mask4).astype(BF)
+    for f in every:
+        v = act(join_columns(dot(t_rec4[...], three_rows_alone(xa4[f], 16)), C4, 16))
+        xa4[f + 1, C4:] = (v * mask4).astype(BF)
+    final[...] = xa4[FRAMES, C4:]
+
     d3 = []
     for f in every:
-        both = jnp.concatenate([dot(keep4[f], u3[...]).astype(BF), keep3[f]], 0)
+        skip3 = jnp.concatenate([xa3[f + 1, 2, C3:][:, 128:], xa3[f + 1, 3, C3:][:, :128]], 1)
+        both = jnp.concatenate([dot(xa4[f + 1, C4:], u3[...]).astype(BF), skip3], 0)
         v = act(join_columns(dot(t_dec3[...], three_rows_alone(both, 32)), C3, 32))
         d3.append((v * mask3d).astype(BF))
 
@@ -654,15 +671,13 @@
         out_specs=(vmem, vmem),
         scratch_shapes=[
             pltpu.VMEM((22, BLOCK, 256), BF),
-            pltpu.VMEM((2, 19, 2 * C2, 256), BF),
-            pltpu.VMEM((2, 6, 2 * C3, 256), BF),
-            pltpu.VMEM((6, C2, 256), BF),
-            pltpu.VMEM((2 * C4, 256), BF),
+            pltpu.VMEM((2, 21, 6 * C2, 256), BF),
+            pltpu.VMEM((FRAMES + 1, 6, 2 * C3, 256), BF),
+            pltpu.VMEM((FRAMES, 6, C2, 256), BF),
+            pltpu.VMEM((FRAMES + 1, 2 * C4, 256), BF),
             pltpu.VMEM((FRAMES, 12, C1 + C2, 128), BF),
             pltpu.VMEM((FRAMES, 20, C0 + C1, 256), BF),
             pltpu.VMEM((FRAMES, 18, C0, 256), BF),
-            pltpu.VMEM((FRAMES, C4, 256), BF),
-            pltpu.VMEM((FRAMES, C3, 256), BF),
             pltpu.VMEM((FRAMES, 3, C2, 256), BF),
         ],
         compiler_params=params,

time: 114 us -> 112 us (0.982)
  Pallas kernels: 50.6 us -> 49 us
    pallas_call x1, Pallas kernels: 31.9 us -> 30.2 us  [per_device(): pl.pallas_call(deep_kernel, out_shape=(jax.ShapeDtypeStruct((FRAMES, 3, 1...]
where the time goes in v1:
time: 112 us
  Pallas kernels  49 us (44%)
  starting transfers between devices  19.7 us (18%)
  waiting for transfers between devices  14.8 us (13%)
  blocking collectives  14.4 us (13%)
  local copies, waits for them, and re-layouts  11.5 us (10%)
  other arithmetic  1.31 us (1%)
    pallas_call x1, Pallas kernels, per_device(): pl.pallas_call(deep_kernel, out_shape=(jax.ShapeDtypeStruct((FRAMES, 3, 1...  30.2 us
    ppermute x6, starting transfers between devices, shifted(): return lax.ppermute(value, axis, pairs)  19.7 us
    ppermute x6, waiting for transfers between devices, shifted(): return lax.ppermute(value, axis, pairs)  14.8 us
    all_gather x1, blocking collectives, per_device(): tile = lax.all_gather(block, 'grp', axis=0)  14.4 us
    pallas_call x1, Pallas kernels, per_device(): pl.pallas_call(fine_kernel, out_shape=(jax.ShapeDtypeStruct((BLOCK, 256),...  12 us
    unnamed x46, local copies, waits for them, and re-layouts  9.13 us
    pallas_call x1, Pallas kernels, per_device(): pl.pallas_call(weights_kernel, out_shape=[jax.ShapeDtypeStruct(taps_shape...  4.74 us
  transfers between devices with their start and end apart: 6, of which 3 were waited for; matrix products, arithmetic and copies ran while one was open for 6% of the time, Pallas kernels for 6%

profile of v1, /device:TPU:106, one launch (start us, length us, event | category | flops | bytes accessed | tf_op | source)
XLA Modules:
  0.0 111.7 jit_solution(5477953776690455059)
XLA Ops:
  0.6 1.1 copy.61
  1.7 1.0 copy.66
  2.7 0.0 copy-start.8
  2.7 0.1 pad.21
  2.8 0.0 copy-start.10
  2.9 0.1 copy.47
  2.9 0.0 copy-start.11
  3.0 0.0 copy-start.12
  3.0 0.0 copy-start.13
  3.0 0.0 copy-start.16
  3.1 0.0 copy-start.17
  3.1 0.0 copy-start.14
  3.1 0.0 copy-start.15
  3.1 3.5 %collective-permute-start = (bf16[1216,256]{1,0:T(8,128)(2,1)S(1)}, bf16[1216,256]{1,0:T(8,128)(2,1)S(1)}, u32[]{:S(2)}, u32[]{:S(2)}) collective-permute-start(bf16[1216,256]{1,0:T(8,128)(2,1)S(1)} %pad_maximum_fusion.own), channel_id=1, source_target_pairs={{0,1},{1,2},{2,3},{3,4},{4,5},{5,6},{6,7},{7,8},{8,9},{9,10},{10,1... | collective-permute-start | bytes 1867784 | tf_op jit(solution)/shard_map/ppermute | solution.py:573
  6.6 2.4 %collective-permute-start.1 = (bf16[1216,256]{1,0:T(8,128)(2,1)S(1)}, bf16[1216,256]{1,0:T(8,128)(2,1)S(1)}, u32[]{:S(2)}, u32[]{:S(2)}) collective-permute-start(bf16[1216,256]{1,0:T(8,128)(2,1)S(1)} %pad_maximum_fusion.own), channel_id=1, source_target_pairs={{1,0},{2,1},{3,2},{4,3},{5,4},{6,5},{7,6},{8,7},{9,8},{10,9},{11,1... | collective-permute-start | bytes 1867784 | tf_op jit(solution)/shard_map/ppermute | solution.py:573
  9.1 1.0 copy.58.refs_7_
  10.1 0.9 copy.59.refs_8_
  11.0 0.9 copy.57.refs_6_
  11.9 0.8 copy.56.refs_4_
  12.7 0.8 copy.55.refs_2_
  13.5 0.8 copy.54.refs_0_
  14.3 0.1 copy.49
  14.4 0.1 copy.51
  14.5 0.1 copy.53
  14.6 0.0 copy-done.15
  14.6 0.1 reshape.47
  14.8 0.1 concatenate.10
  14.9 4.7 %weights.1 = (bf16[128,144]{1,0:T(8,128)(2,1)}, bf16[192,256]{1,0:T(8,128)(2,1)}, bf16[144,96]{1,0:T(8,128)(2,1)}, bf16[144,288]{1,0:T(8,128)(2,1)}, bf16[192,14...) custom-call(bf16[9,32,7]{2,1,0:T(8,128)(2,1)} %copy.54.refs_0_, ...), custom_call_target="tpu_custom_call" | custom-call | bytes 20000000 | tf_op jit(solution)/shard_map/weights/pallas_call | solution.py:621
  19.7 0.6 pad_add_fusion.pos
  20.3 0.6 fusion.1.rest
  20.9 0.0 collective-permute-done.up
  21.0 3.1 %collective-permute-done.1.down = bf16[1216,256]{1,0:T(8,128)(2,1)S(1)} collective-permute-done((bf16[1216,256]{1,0:T(8,128)(2,1)S(1)}, bf16[1216,256]{1,0:T(8,128)(2,1)S(1)}, u32[]{:S(2)}, u32[]{:S(2)}) %collective-permute-start.1) | collective-permute-done | bytes 622624 | tf_op jit(solution)/shard_map/ppermute | solution.py:573
  24.0 0.8 copy-done.5
  24.8 12.0 %fine.1 = (bf16[304,256]{1,0:T(8,128)(2,1)}, bf16[4,20,32,256]{3,2,1,0:T(8,128)(2,1)}, bf16[4,12,48,128]{3,2,1,0:T(8,128)(2,1)}) custom-call(s32[2]{0:T(128)} %pad_add_fusion.pos, bf16[1216,256]{1,0:T(8,128)(2,1)} %copy-done.1, bf16[1216,256]{1,0:T(8,128)(2,1)} %copy-done.4, bf16[1216,256]{1,0:T(8,128)(2,1)} %copy-done.5, bf16[112,256]{1,0:T(8,128)(2,1)} %fusion.1.rest, ...), custom_call_target="tpu_custom_call" | custom-call | tf_op jit(solution)/shard_map/fine/pallas_call | solution.py:630
  36.8 14.4 %all-gather = bf16[1216,256]{1,0:T(8,128)(2,1)S(1)} all-gather(bf16[304,256]{1,0:T(8,128)(2,1)} %get-tuple-element.28), channel_id=2, replica_groups=mesh['tile'=64,'grp'=4] {'grp'}, dimensions={0}, use_global_device_ids=true | all-gather | bytes 778240 | tf_op jit(solution)/shard_map/all_gather | solution.py:650
  51.2 1.9 %collective-permute-start.2 = (bf16[4,304,256]{2,1,0:T(8,128)(2,1)S(1)}, bf16[4,304,256]{2,1,0:T(8,128)(2,1)S(1)}, u32[]{:S(2)}, u32[]{:S(2)}) collective-permute-start(bf16[4,304,256]{2,1,0:T(8,128)(2,1)S(1)} %bitcast.26), channel_id=1, source_target_pairs={{0,4},{4,8},{8,12},{12,16},{16,20},{20,24},{24,28},{28,32},{32,36}... | collective-permute-start | bytes 1867784 | tf_op jit(solution)/shard_map/ppermute | solution.py:573
  53.1 3.6 %collective-permute-start.3 = (bf16[4,304,256]{2,1,0:T(8,128)(2,1)S(1)}, bf16[4,304,256]{2,1,0:T(8,128)(2,1)S(1)}, u32[]{:S(2)}, u32[]{:S(2)}) collective-permute-start(bf16[4,304,256]{2,1,0:T(8,128)(2,1)S(1)} %bitcast.27), channel_id=1, source_target_pairs={{4,0},{8,4},{12,8},{16,12},{20,16},{24,20},{28,24},{32,28},{36,32}... | collective-permute-start | bytes 1867784 | tf_op jit(solution)/shard_map/ppermute | solution.py:573
  56.8 2.1 %pack.1 = (bf16[880,256]{1,0:T(8,128)(2,1)}, bf16[880,256]{1,0:T(8,128)(2,1)}) custom-call(bf16[4,304,256]{2,1,0:T(8,128)(2,1)} %bitcast.28), custom_call_target="tpu_custom_call" | custom-call | tf_op jit(solution)/shard_map/pack/pallas_call | solution.py:655
  58.8 6.3 %collective-permute-start.4 = (bf16[880,256]{1,0:T(8,128)(2,1)}, bf16[880,256]{1,0:T(8,128)(2,1)S(1)}, u32[]{:S(2)}, u32[]{:S(2)}) collective-permute-start(bf16[880,256]{1,0:T(8,128)(2,1)} %get-tuple-element.29), channel_id=1, source_target_pairs={{0,8},{4,12},{8,16},{12,20},{16,24},{20,28},{24,32},{28,36},{32,40... | collective-permute-start | bytes 1351688 | tf_op jit(solution)/shard_map/ppermute | solution.py:573
  65.1 1.9 %collective-permute-start.5 = (bf16[880,256]{1,0:T(8,128)(2,1)}, bf16[880,256]{1,0:T(8,128)(2,1)S(1)}, u32[]{:S(2)}, u32[]{:S(2)}) collective-permute-start(bf16[880,256]{1,0:T(8,128)(2,1)} %get-tuple-element.30), channel_id=1, source_target_pairs={{8,0},{12,4},{16,8},{20,12},{24,16},{28,20},{32,24},{36,28},{40,32... | collective-permute-start | bytes 1351688 | tf_op jit(solution)/shard_map/ppermute | solution.py:573
  67.1 6.9 %collective-permute-done.4.up2 = bf16[880,256]{1,0:T(8,128)(2,1)S(1)} collective-permute-done((bf16[880,256]{1,0:T(8,128)(2,1)}, bf16[880,256]{1,0:T(8,128)(2,1)S(1)}, u32[]{:S(2)}, u32[]{:S(2)}) %collective-permute-start.4) | collective-permute-done | bytes 450592 | tf_op jit(solution)/shard_map/ppermute | solution.py:573
  74.0 4.9 %collective-permute-done.5.down2 = bf16[880,256]{1,0:T(8,128)(2,1)S(1)} collective-permute-done((bf16[880,256]{1,0:T(8,128)(2,1)}, bf16[880,256]{1,0:T(8,128)(2,1)S(1)}, u32[]{:S(2)}, u32[]{:S(2)}) %collective-permute-start.5) | collective-permute-done | bytes 450592 | tf_op jit(solution)/shard_map/ppermute | solution.py:573
  78.9 0.7 copy-done.7
  79.6 0.2 copy-done.2
  79.8 0.2 copy-done.3
  80.0 30.2 %deep.1 = (f32[4,3,16,256]{3,2,1,0:T(8,128)}, bf16[112,256]{1,0:T(8,128)(2,1)}) custom-call(s32[2]{0:T(128)} %pad_add_fusion.pos, bf16[4,304,256]{2,1,0:T(8,128)(2,1)} %bitcast.29, bf16[4,304,256]{2,1,0:T(8,128)(2,1)} %copy-done.2, bf16[4,304,256]{2,1,0:T(8,128)(2,1)} %copy-done.3, bf16[880,256]{1,0:T(8,128)(2,1)} %copy-done.6, bf16[880,256]{1,0:T(8,128)(2,1)} %copy-done.7, ...), custom_call_target="tpu_custom_call" | custom-call | tf_op jit(solution)/shard_map/deep/pallas_call | solution.py:664
  110.3 0.7 slice_bitcast_fusion
  111.0 0.7 copy.60
  (32 shorter events, 0.2 us)
Async XLA Ops:
  0.6 2.2 %copy-start.9 = (bf16[32,16,256]{2,1,0:T(8,128)(2,1)S(1)}, bf16[32,16,256]{2,1,0:T(8,128)(2,1)}, u32[]{:S(2)}) copy-start(bf16[32,16,256]{2,1,0:T(8,128)(2,1)} %param.30) | copy-start | bytes 786436
  2.7 6.4 %copy-start.8 = (bf16[9,76,152]{1,2,0:T(8,128)(2,1)S(1)}, bf16[9,76,152]{1,2,0:T(8,128)(2,1)}, u32[]{:S(2)}) copy-start(bf16[9,76,152]{1,2,0:T(8,128)(2,1)} %param.43) | copy-start | bytes 623812
  2.8 7.3 %copy-start.10 = (bf16[9,101,76]{1,2,0:T(8,128)(2,1)S(1)}, bf16[9,101,76]{1,2,0:T(8,128)(2,1)}, u32[]{:S(2)}) copy-start(bf16[9,101,76]{1,2,0:T(8,128)(2,1)} %param.39) | copy-start | bytes 414508
  2.9 8.1 %copy-start.11 = (bf16[9,76,57]{1,2,0:T(8,128)(2,1)S(1)}, bf16[9,76,57]{1,2,0:T(8,128)(2,1)}, u32[]{:S(2)}) copy-start(bf16[9,76,57]{1,2,0:T(8,128)(2,1)} %param.38) | copy-start | bytes 233932
  3.0 8.9 %copy-start.12 = (bf16[9,57,43]{1,2,0:T(8,128)(2,1)S(1)}, bf16[9,57,43]{1,2,0:T(8,128)(2,1)}, u32[]{:S(2)}) copy-start(bf16[9,57,43]{1,2,0:T(8,128)(2,1)} %param.37) | copy-start | bytes 132358
  3.0 9.8 %copy-start.13 = (bf16[9,43,32]{1,2,0:T(8,128)(2,1)S(1)}, bf16[9,43,32]{1,2,0:T(8,128)(2,1)}, u32[]{:S(2)}) copy-start(bf16[9,43,32]{1,2,0:T(8,128)(2,1)} %param.36) | copy-start | bytes 74308
  3.0 11.9 %copy-start.1 = (bf16[1216,256]{1,0:T(8,128)(2,1)}, bf16[1216,256]{1,0:T(8,128)(2,1)S(1)}, u32[]{:S(2)}) copy-start(bf16[1216,256]{1,0:T(8,128)(2,1)S(1)} %pad_maximum_fusion.own) | copy-start | bytes 1867780
  3.0 10.5 %copy-start.16 = (bf16[9,32,7]{1,2,0:T(8,128)(2,1)S(1)}, bf16[9,32,7]{1,2,0:T(8,128)(2,1)}, u32[]{:S(2)}) copy-start(bf16[9,32,7]{1,2,0:T(8,128)(2,1)} %param.35) | copy-start | bytes 12100
  3.1 11.2 %copy-start.17 = (bf16[101,1,16]{0,2,1:T(8,128)(2,1)S(1)}, bf16[101,1,16]{0,2,1:T(8,128)(2,1)}, u32[]{:S(2)}) copy-start(bf16[101,1,16]{0,2,1:T(8,128)(2,1)} %param.34) | copy-start | bytes 9700
  3.1 11.3 %copy-start.14 = (bf16[76,2,32]{0,2,1:T(8,128)(2,1)S(1)}, bf16[76,2,32]{0,2,1:T(8,128)(2,1)}, u32[]{:S(2)}) copy-start(bf16[76,2,32]{0,2,1:T(8,128)(2,1)} %param.33) | copy-start | bytes 29188
  3.1 11.5 %copy-start.15 = (bf16[57,4,64]{2,1,0:T(4,128)(2,1)S(1)}, bf16[57,4,64]{2,1,0:T(4,128)(2,1)}, u32[]{:S(2)}) copy-start(bf16[57,4,64]{2,1,0:T(4,128)(2,1)} %param.32) | copy-start | bytes 87556
  3.1 17.9 %collective-permute-start = (bf16[1216,256]{1,0:T(8,128)(2,1)S(1)}, bf16[1216,256]{1,0:T(8,128)(2,1)S(1)}, u32[]{:S(2)}, u32[]{:S(2)}) collective-permute-start(bf16[1216,256]{1,0:T(8,128)(2,1)S(1)} %pad_maximum_fusion.own), channel_id=1, source_target_pairs={{0,1},{1,2},{2,3},{3,4},{4,5},{5,6},{6,7},{7,8},{8,9},{9,10},{10,1... | collective-permute-start | bytes 1867784 | tf_op jit(solution)/shard_map/ppermute | solution.py:573
  6.6 17.4 %collective-permute-start.1 = (bf16[1216,256]{1,0:T(8,128)(2,1)S(1)}, bf16[1216,256]{1,0:T(8,128)(2,1)S(1)}, u32[]{:S(2)}, u32[]{:S(2)}) collective-permute-start(bf16[1216,256]{1,0:T(8,128)(2,1)S(1)} %pad_maximum_fusion.own), channel_id=1, source_target_pairs={{1,0},{2,1},{3,2},{4,3},{5,4},{6,5},{7,6},{8,7},{9,8},{10,9},{11,1... | collective-permute-start | bytes 1867784 | tf_op jit(solution)/shard_map/ppermute | solution.py:573
  20.9 3.1 %copy-start.4 = (bf16[1216,256]{1,0:T(8,128)(2,1)}, bf16[1216,256]{1,0:T(8,128)(2,1)S(1)}, u32[]{:S(2)}) copy-start(bf16[1216,256]{1,0:T(8,128)(2,1)S(1)} %collective-permute-done.up) | copy-start | bytes 1867780
  24.0 0.8 copy-start.5
  51.2 5.6 %copy-start = (bf16[1216,256]{1,0:T(8,128)(2,1)}, bf16[1216,256]{1,0:T(8,128)(2,1)S(1)}, u32[]{:S(2)}) copy-start(bf16[1216,256]{1,0:T(8,128)(2,1)S(1)} %all-gather) | copy-start | bytes 1867780
  51.2 27.6 %collective-permute-start.2 = (bf16[4,304,256]{2,1,0:T(8,128)(2,1)S(1)}, bf16[4,304,256]{2,1,0:T(8,128)(2,1)S(1)}, u32[]{:S(2)}, u32[]{:S(2)}) collective-permute-start(bf16[4,304,256]{2,1,0:T(8,128)(2,1)S(1)} %bitcast.26), channel_id=1, source_target_pairs={{0,4},{4,8},{8,12},{12,16},{16,20},{20,24},{24,28},{28,32},{32,36}... | collective-permute-start | bytes 1867784 | tf_op jit(solution)/shard_map/ppermute | solution.py:573
  53.1 25.7 %collective-permute-start.3 = (bf16[4,304,256]{2,1,0:T(8,128)(2,1)S(1)}, bf16[4,304,256]{2,1,0:T(8,128)(2,1)S(1)}, u32[]{:S(2)}, u32[]{:S(2)}) collective-permute-start(bf16[4,304,256]{2,1,0:T(8,128)(2,1)S(1)} %bitcast.27), channel_id=1, source_target_pairs={{4,0},{8,4},{12,8},{16,12},{20,16},{24,20},{28,24},{32,28},{36,32}... | collective-permute-start | bytes 1867784 | tf_op jit(solution)/shard_map/ppermute | solution.py:573
  58.8 15.1 %collective-permute-start.4 = (bf16[880,256]{1,0:T(8,128)(2,1)}, bf16[880,256]{1,0:T(8,128)(2,1)S(1)}, u32[]{:S(2)}, u32[]{:S(2)}) collective-permute-start(bf16[880,256]{1,0:T(8,128)(2,1)} %get-tuple-element.29), channel_id=1, source_target_pairs={{0,8},{4,12},{8,16},{12,20},{16,24},{20,28},{24,32},{28,36},{32,40... | collective-permute-start | bytes 1351688 | tf_op jit(solution)/shard_map/ppermute | solution.py:573
  65.1 13.7 %collective-permute-start.5 = (bf16[880,256]{1,0:T(8,128)(2,1)}, bf16[880,256]{1,0:T(8,128)(2,1)S(1)}, u32[]{:S(2)}, u32[]{:S(2)}) collective-permute-start(bf16[880,256]{1,0:T(8,128)(2,1)} %get-tuple-element.30), channel_id=1, source_target_pairs={{8,0},{12,4},{16,8},{20,12},{24,16},{28,20},{32,24},{36,28},{40,32... | collective-permute-start | bytes 1351688 | tf_op jit(solution)/shard_map/ppermute | solution.py:573
  74.0 4.9 %copy-start.6 = (bf16[880,256]{1,0:T(8,128)(2,1)}, bf16[880,256]{1,0:T(8,128)(2,1)S(1)}, u32[]{:S(2)}) copy-start(bf16[880,256]{1,0:T(8,128)(2,1)S(1)} %collective-permute-done.4.up2) | copy-start | bytes 1351684
  78.8 0.8 copy-start.7
  78.8 1.0 copy-start.2
  78.8 1.2 %copy-start.3 = (bf16[4,304,256]{2,1,0:T(8,128)(2,1)}, bf16[4,304,256]{2,1,0:T(8,128)(2,1)S(1)}, u32[]{:S(2)}) copy-start(bf16[4,304,256]{2,1,0:T(8,128)(2,1)S(1)} %collective-permute-done.3.down1) | copy-start | bytes 1867780

commit v2 on v1

--- a/solution.py
+++ b/solution.py
@@ -19,7 +19,7 @@
 PREFIX = (X_AT[0] + C1, X_AT[1] + C1, X_AT[2] + C1, X_AT[3] + C1)
 VMEM = 56 * 1024 * 1024
 GROUP = 12
-GROUP2 = 6
+GROUP2 = 8
 
 
 SHAPES = {

time: 112 us -> 118 us (1.054)
  Pallas kernels: 49 us -> 54.8 us
    pallas_call x1, Pallas kernels: 30.2 us -> 36 us  [per_device(): pl.pallas_call(deep_kernel, out_shape=(jax.ShapeDtypeStruct((FRAMES, 3, 1...]
where the time goes in v2:
time: 118 us; the launch traced here: 117 us
  Pallas kernels  54.8 us (46%)
  starting transfers between devices  19.6 us (17%)
  waiting for transfers between devices  15 us (13%)
  blocking collectives  14.4 us (12%)
  local copies, waits for them, and re-layouts  11.5 us (10%)
  other arithmetic  1.31 us (1%)
    pallas_call x1, Pallas kernels, per_device(): pl.pallas_call(deep_kernel, out_shape=(jax.ShapeDtypeStruct((FRAMES, 3, 1...  36 us
    ppermute x6, starting transfers between devices, shifted(): return lax.ppermute(value, axis, pairs)  19.6 us
    ppermute x6, waiting for transfers between devices, shifted(): return lax.ppermute(value, axis, pairs)  15 us
    all_gather x1, blocking collectives, per_device(): tile = lax.all_gather(block, 'grp', axis=0)  14.4 us
    pallas_call x1, Pallas kernels, per_device(): pl.pallas_call(fine_kernel, out_shape=(jax.ShapeDtypeStruct((BLOCK, 256),...  12 us
    unnamed x46, local copies, waits for them, and re-layouts  9.13 us
    pallas_call x1, Pallas kernels, per_device(): pl.pallas_call(weights_kernel, out_shape=[jax.ShapeDtypeStruct(taps_shape...  4.74 us
  transfers between devices with their start and end apart: 6, of which 3 were waited for; matrix products, arithmetic and copies ran while one was open for 6% of the time, Pallas kernels for 6%

profile of v2, /device:TPU:106, one launch (start us, length us, event | category | flops | bytes accessed | tf_op | source)
XLA Modules:
  0.0 117.5 jit_solution(1899322829628736324)
XLA Ops:
  0.6 1.1 copy.61
  1.7 1.0 copy.66
  2.7 0.0 copy-start.8
  2.7 0.1 pad.21
  2.8 0.0 copy-start.10
  2.9 0.1 copy.47
  2.9 0.0 copy-start.11
  3.0 0.0 copy-start.12
  3.0 0.0 copy-start.13
  3.0 0.0 copy-start.16
  3.1 0.0 copy-start.17
  3.1 0.0 copy-start.14
  3.1 0.0 copy-start.15
  3.1 3.5 %collective-permute-start = (bf16[1216,256]{1,0:T(8,128)(2,1)S(1)}, bf16[1216,256]{1,0:T(8,128)(2,1)S(1)}, u32[]{:S(2)}, u32[]{:S(2)}) collective-permute-start(bf16[1216,256]{1,0:T(8,128)(2,1)S(1)} %pad_maximum_fusion.own), channel_id=1, source_target_pairs={{0,1},{1,2},{2,3},{3,4},{4,5},{5,6},{6,7},{7,8},{8,9},{9,10},{10,1... | collective-permute-start | bytes 1867784 | tf_op jit(solution)/shard_map/ppermute | solution.py:573
  6.6 2.4 %collective-permute-start.1 = (bf16[1216,256]{1,0:T(8,128)(2,1)S(1)}, bf16[1216,256]{1,0:T(8,128)(2,1)S(1)}, u32[]{:S(2)}, u32[]{:S(2)}) collective-permute-start(bf16[1216,256]{1,0:T(8,128)(2,1)S(1)} %pad_maximum_fusion.own), channel_id=1, source_target_pairs={{1,0},{2,1},{3,2},{4,3},{5,4},{6,5},{7,6},{8,7},{9,8},{10,9},{11,1... | collective-permute-start | bytes 1867784 | tf_op jit(solution)/shard_map/ppermute | solution.py:573
  9.1 1.0 copy.58.refs_7_
  10.1 0.9 copy.59.refs_8_
  11.0 0.9 copy.57.refs_6_
  11.9 0.8 copy.56.refs_4_
  12.7 0.8 copy.55.refs_2_
  13.5 0.8 copy.54.refs_0_
  14.3 0.1 copy.49
  14.4 0.1 copy.51
  14.5 0.1 copy.53
  14.6 0.0 copy-done.15
  14.6 0.1 reshape.47
  14.8 0.1 concatenate.10
  14.9 4.7 %weights.1 = (bf16[128,144]{1,0:T(8,128)(2,1)}, bf16[192,256]{1,0:T(8,128)(2,1)}, bf16[144,96]{1,0:T(8,128)(2,1)}, bf16[144,288]{1,0:T(8,128)(2,1)}, bf16[192,14...) custom-call(bf16[9,32,7]{2,1,0:T(8,128)(2,1)} %copy.54.refs_0_, ...), custom_call_target="tpu_custom_call" | custom-call | bytes 20000000 | tf_op jit(solution)/shard_map/weights/pallas_call | solution.py:621
  19.7 0.6 pad_add_fusion.pos
  20.3 0.6 fusion.1.rest
  20.9 0.0 collective-permute-done.up
  21.0 3.1 %collective-permute-done.1.down = bf16[1216,256]{1,0:T(8,128)(2,1)S(1)} collective-permute-done((bf16[1216,256]{1,0:T(8,128)(2,1)S(1)}, bf16[1216,256]{1,0:T(8,128)(2,1)S(1)}, u32[]{:S(2)}, u32[]{:S(2)}) %collective-permute-start.1) | collective-permute-done | bytes 622624 | tf_op jit(solution)/shard_map/ppermute | solution.py:573
  24.0 0.8 copy-done.5
  24.8 12.0 %fine.1 = (bf16[304,256]{1,0:T(8,128)(2,1)}, bf16[4,20,32,256]{3,2,1,0:T(8,128)(2,1)}, bf16[4,12,48,128]{3,2,1,0:T(8,128)(2,1)}) custom-call(s32[2]{0:T(128)} %pad_add_fusion.pos, bf16[1216,256]{1,0:T(8,128)(2,1)} %copy-done.1, bf16[1216,256]{1,0:T(8,128)(2,1)} %copy-done.4, bf16[1216,256]{1,0:T(8,128)(2,1)} %copy-done.5, bf16[112,256]{1,0:T(8,128)(2,1)} %fusion.1.rest, ...), custom_call_target="tpu_custom_call" | custom-call | tf_op jit(solution)/shard_map/fine/pallas_call | solution.py:630
  36.8 14.4 %all-gather = bf16[1216,256]{1,0:T(8,128)(2,1)S(1)} all-gather(bf16[304,256]{1,0:T(8,128)(2,1)} %get-tuple-element.28), channel_id=2, replica_groups=mesh['tile'=64,'grp'=4] {'grp'}, dimensions={0}, use_global_device_ids=true | all-gather | bytes 778240 | tf_op jit(solution)/shard_map/all_gather | solution.py:650
  51.2 1.9 %collective-permute-start.2 = (bf16[4,304,256]{2,1,0:T(8,128)(2,1)S(1)}, bf16[4,304,256]{2,1,0:T(8,128)(2,1)S(1)}, u32[]{:S(2)}, u32[]{:S(2)}) collective-permute-start(bf16[4,304,256]{2,1,0:T(8,128)(2,1)S(1)} %bitcast.26), channel_id=1, source_target_pairs={{0,4},{4,8},{8,12},{12,16},{16,20},{20,24},{24,28},{28,32},{32,36}... | collective-permute-start | bytes 1867784 | tf_op jit(solution)/shard_map/ppermute | solution.py:573
  53.1 3.6 %collective-permute-start.3 = (bf16[4,304,256]{2,1,0:T(8,128)(2,1)S(1)}, bf16[4,304,256]{2,1,0:T(8,128)(2,1)S(1)}, u32[]{:S(2)}, u32[]{:S(2)}) collective-permute-start(bf16[4,304,256]{2,1,0:T(8,128)(2,1)S(1)} %bitcast.27), channel_id=1, source_target_pairs={{4,0},{8,4},{12,8},{16,12},{20,16},{24,20},{28,24},{32,28},{36,32}... | collective-permute-start | bytes 1867784 | tf_op jit(solution)/shard_map/ppermute | solution.py:573
  56.8 2.1 %pack.1 = (bf16[880,256]{1,0:T(8,128)(2,1)}, bf16[880,256]{1,0:T(8,128)(2,1)}) custom-call(bf16[4,304,256]{2,1,0:T(8,128)(2,1)} %bitcast.28), custom_call_target="tpu_custom_call" | custom-call | tf_op jit(solution)/shard_map/pack/pallas_call | solution.py:655
  58.8 6.1 %collective-permute-start.4 = (bf16[880,256]{1,0:T(8,128)(2,1)}, bf16[880,256]{1,0:T(8,128)(2,1)S(1)}, u32[]{:S(2)}, u32[]{:S(2)}) collective-permute-start(bf16[880,256]{1,0:T(8,128)(2,1)} %get-tuple-element.29), channel_id=1, source_target_pairs={{0,8},{4,12},{8,16},{12,20},{16,24},{20,28},{24,32},{28,36},{32,40... | collective-permute-start | bytes 1351688 | tf_op jit(solution)/shard_map/ppermute | solution.py:573
  65.0 1.9 %collective-permute-start.5 = (bf16[880,256]{1,0:T(8,128)(2,1)}, bf16[880,256]{1,0:T(8,128)(2,1)S(1)}, u32[]{:S(2)}, u32[]{:S(2)}) collective-permute-start(bf16[880,256]{1,0:T(8,128)(2,1)} %get-tuple-element.30), channel_id=1, source_target_pairs={{8,0},{12,4},{16,8},{20,12},{24,16},{28,20},{32,24},{36,28},{40,32... | collective-permute-start | bytes 1351688 | tf_op jit(solution)/shard_map/ppermute | solution.py:573
  66.9 6.9 %collective-permute-done.4.up2 = bf16[880,256]{1,0:T(8,128)(2,1)S(1)} collective-permute-done((bf16[880,256]{1,0:T(8,128)(2,1)}, bf16[880,256]{1,0:T(8,128)(2,1)S(1)}, u32[]{:S(2)}, u32[]{:S(2)}) %collective-permute-start.4) | collective-permute-done | bytes 450592 | tf_op jit(solution)/shard_map/ppermute | solution.py:573
  73.8 5.0 %collective-permute-done.5.down2 = bf16[880,256]{1,0:T(8,128)(2,1)S(1)} collective-permute-done((bf16[880,256]{1,0:T(8,128)(2,1)}, bf16[880,256]{1,0:T(8,128)(2,1)S(1)}, u32[]{:S(2)}, u32[]{:S(2)}) %collective-permute-start.5) | collective-permute-done | bytes 450592 | tf_op jit(solution)/shard_map/ppermute | solution.py:573
  78.9 0.7 copy-done.7
  79.6 0.2 copy-done.2
  79.8 0.2 copy-done.3
  80.0 36.0 %deep.1 = (f32[4,3,16,256]{3,2,1,0:T(8,128)}, bf16[112,256]{1,0:T(8,128)(2,1)}) custom-call(s32[2]{0:T(128)} %pad_add_fusion.pos, bf16[4,304,256]{2,1,0:T(8,128)(2,1)} %bitcast.29, bf16[4,304,256]{2,1,0:T(8,128)(2,1)} %copy-done.2, bf16[4,304,256]{2,1,0:T(8,128)(2,1)} %copy-done.3, bf16[880,256]{1,0:T(8,128)(2,1)} %copy-done.6, bf16[880,256]{1,0:T(8,128)(2,1)} %copy-done.7, ...), custom_call_target="tpu_custom_call" | custom-call | tf_op jit(solution)/shard_map/deep/pallas_call | solution.py:664
  116.0 0.7 slice_bitcast_fusion
  116.8 0.7 copy.60
  (32 shorter events, 0.2 us)
Async XLA Ops:
  0.6 2.2 %copy-start.9 = (bf16[32,16,256]{2,1,0:T(8,128)(2,1)S(1)}, bf16[32,16,256]{2,1,0:T(8,128)(2,1)}, u32[]{:S(2)}) copy-start(bf16[32,16,256]{2,1,0:T(8,128)(2,1)} %param.30) | copy-start | bytes 786436
  2.7 6.4 %copy-start.8 = (bf16[9,76,152]{1,2,0:T(8,128)(2,1)S(1)}, bf16[9,76,152]{1,2,0:T(8,128)(2,1)}, u32[]{:S(2)}) copy-start(bf16[9,76,152]{1,2,0:T(8,128)(2,1)} %param.43) | copy-start | bytes 623812
  2.8 7.3 %copy-start.10 = (bf16[9,101,76]{1,2,0:T(8,128)(2,1)S(1)}, bf16[9,101,76]{1,2,0:T(8,128)(2,1)}, u32[]{:S(2)}) copy-start(bf16[9,101,76]{1,2,0:T(8,128)(2,1)} %param.39) | copy-start | bytes 414508
  2.9 8.1 %copy-start.11 = (bf16[9,76,57]{1,2,0:T(8,128)(2,1)S(1)}, bf16[9,76,57]{1,2,0:T(8,128)(2,1)}, u32[]{:S(2)}) copy-start(bf16[9,76,57]{1,2,0:T(8,128)(2,1)} %param.38) | copy-start | bytes 233932
  3.0 8.9 %copy-start.12 = (bf16[9,57,43]{1,2,0:T(8,128)(2,1)S(1)}, bf16[9,57,43]{1,2,0:T(8,128)(2,1)}, u32[]{:S(2)}) copy-start(bf16[9,57,43]{1,2,0:T(8,128)(2,1)} %param.37) | copy-start | bytes 132358
  3.0 9.8 %copy-start.13 = (bf16[9,43,32]{1,2,0:T(8,128)(2,1)S(1)}, bf16[9,43,32]{1,2,0:T(8,128)(2,1)}, u32[]{:S(2)}) copy-start(bf16[9,43,32]{1,2,0:T(8,128)(2,1)} %param.36) | copy-start | bytes 74308
  3.0 11.9 %copy-start.1 = (bf16[1216,256]{1,0:T(8,128)(2,1)}, bf16[1216,256]{1,0:T(8,128)(2,1)S(1)}, u32[]{:S(2)}) copy-start(bf16[1216,256]{1,0:T(8,128)(2,1)S(1)} %pad_maximum_fusion.own) | copy-start | bytes 1867780
  3.0 10.5 %copy-start.16 = (bf16[9,32,7]{1,2,0:T(8,128)(2,1)S(1)}, bf16[9,32,7]{1,2,0:T(8,128)(2,1)}, u32[]{:S(2)}) copy-start(bf16[9,32,7]{1,2,0:T(8,128)(2,1)} %param.35) | copy-start | bytes 12100
  3.1 11.2 %copy-start.17 = (bf16[101,1,16]{0,2,1:T(8,128)(2,1)S(1)}, bf16[101,1,16]{0,2,1:T(8,128)(2,1)}, u32[]{:S(2)}) copy-start(bf16[101,1,16]{0,2,1:T(8,128)(2,1)} %param.34) | copy-start | bytes 9700
  3.1 11.3 %copy-start.14 = (bf16[76,2,32]{0,2,1:T(8,128)(2,1)S(1)}, bf16[76,2,32]{0,2,1:T(8,128)(2,1)}, u32[]{:S(2)}) copy-start(bf16[76,2,32]{0,2,1:T(8,128)(2,1)} %param.33) | copy-start | bytes 29188
  3.1 11.5 %copy-start.15 = (bf16[57,4,64]{2,1,0:T(4,128)(2,1)S(1)}, bf16[57,4,64]{2,1,0:T(4,128)(2,1)}, u32[]{:S(2)}) copy-start(bf16[57,4,64]{2,1,0:T(4,128)(2,1)} %param.32) | copy-start | bytes 87556
  3.1 17.9 %collective-permute-start = (bf16[1216,256]{1,0:T(8,128)(2,1)S(1)}, bf16[1216,256]{1,0:T(8,128)(2,1)S(1)}, u32[]{:S(2)}, u32[]{:S(2)}) collective-permute-start(bf16[1216,256]{1,0:T(8,128)(2,1)S(1)} %pad_maximum_fusion.own), channel_id=1, source_target_pairs={{0,1},{1,2},{2,3},{3,4},{4,5},{5,6},{6,7},{7,8},{8,9},{9,10},{10,1... | collective-permute-start | bytes 1867784 | tf_op jit(solution)/shard_map/ppermute | solution.py:573
  6.6 17.4 %collective-permute-start.1 = (bf16[1216,256]{1,0:T(8,128)(2,1)S(1)}, bf16[1216,256]{1,0:T(8,128)(2,1)S(1)}, u32[]{:S(2)}, u32[]{:S(2)}) collective-permute-start(bf16[1216,256]{1,0:T(8,128)(2,1)S(1)} %pad_maximum_fusion.own), channel_id=1, source_target_pairs={{1,0},{2,1},{3,2},{4,3},{5,4},{6,5},{7,6},{8,7},{9,8},{10,9},{11,1... | collective-permute-start | bytes 1867784 | tf_op jit(solution)/shard_map/ppermute | solution.py:573
  20.9 3.1 %copy-start.4 = (bf16[1216,256]{1,0:T(8,128)(2,1)}, bf16[1216,256]{1,0:T(8,128)(2,1)S(1)}, u32[]{:S(2)}) copy-start(bf16[1216,256]{1,0:T(8,128)(2,1)S(1)} %collective-permute-done.up) | copy-start | bytes 1867780
  24.0 0.8 copy-start.5
  51.2 5.6 %copy-start = (bf16[1216,256]{1,0:T(8,128)(2,1)}, bf16[1216,256]{1,0:T(8,128)(2,1)S(1)}, u32[]{:S(2)}) copy-start(bf16[1216,256]{1,0:T(8,128)(2,1)S(1)} %all-gather) | copy-start | bytes 1867780
  51.2 27.6 %collective-permute-start.2 = (bf16[4,304,256]{2,1,0:T(8,128)(2,1)S(1)}, bf16[4,304,256]{2,1,0:T(8,128)(2,1)S(1)}, u32[]{:S(2)}, u32[]{:S(2)}) collective-permute-start(bf16[4,304,256]{2,1,0:T(8,128)(2,1)S(1)} %bitcast.26), channel_id=1, source_target_pairs={{0,4},{4,8},{8,12},{12,16},{16,20},{20,24},{24,28},{28,32},{32,36}... | collective-permute-start | bytes 1867784 | tf_op jit(solution)/shard_map/ppermute | solution.py:573
  53.1 25.7 %collective-permute-start.3 = (bf16[4,304,256]{2,1,0:T(8,128)(2,1)S(1)}, bf16[4,304,256]{2,1,0:T(8,128)(2,1)S(1)}, u32[]{:S(2)}, u32[]{:S(2)}) collective-permute-start(bf16[4,304,256]{2,1,0:T(8,128)(2,1)S(1)} %bitcast.27), channel_id=1, source_target_pairs={{4,0},{8,4},{12,8},{16,12},{20,16},{24,20},{28,24},{32,28},{36,32}... | collective-permute-start | bytes 1867784 | tf_op jit(solution)/shard_map/ppermute | solution.py:573
  58.8 15.0 %collective-permute-start.4 = (bf16[880,256]{1,0:T(8,128)(2,1)}, bf16[880,256]{1,0:T(8,128)(2,1)S(1)}, u32[]{:S(2)}, u32[]{:S(2)}) collective-permute-start(bf16[880,256]{1,0:T(8,128)(2,1)} %get-tuple-element.29), channel_id=1, source_target_pairs={{0,8},{4,12},{8,16},{12,20},{16,24},{20,28},{24,32},{28,36},{32,40... | collective-permute-start | bytes 1351688 | tf_op jit(solution)/shard_map/ppermute | solution.py:573
  65.0 13.9 %collective-permute-start.5 = (bf16[880,256]{1,0:T(8,128)(2,1)}, bf16[880,256]{1,0:T(8,128)(2,1)S(1)}, u32[]{:S(2)}, u32[]{:S(2)}) collective-permute-start(bf16[880,256]{1,0:T(8,128)(2,1)} %get-tuple-element.30), channel_id=1, source_target_pairs={{8,0},{12,4},{16,8},{20,12},{24,16},{28,20},{32,24},{36,28},{40,32... | collective-permute-start | bytes 1351688 | tf_op jit(solution)/shard_map/ppermute | solution.py:573
  73.8 5.1 %copy-start.6 = (bf16[880,256]{1,0:T(8,128)(2,1)}, bf16[880,256]{1,0:T(8,128)(2,1)S(1)}, u32[]{:S(2)}) copy-start(bf16[880,256]{1,0:T(8,128)(2,1)S(1)} %collective-permute-done.4.up2) | copy-start | bytes 1351684
  78.8 0.8 copy-start.7
  78.8 1.0 copy-start.2
  78.8 1.2 %copy-start.3 = (bf16[4,304,256]{2,1,0:T(8,128)(2,1)}, bf16[4,304,256]{2,1,0:T(8,128)(2,1)S(1)}, u32[]{:S(2)}) copy-start(bf16[4,304,256]{2,1,0:T(8,128)(2,1)S(1)} %collective-permute-done.3.down1) | copy-start | bytes 1867780
